TPU v7x, 128 devices: a whole 4x4x4 slice. The times are simulated.
128 devices in a mesh: dp: 4 (over x), expert: 32 (over y, z, core).
Axes of the slice: x: 4, y: 4, z: 4, core: 2. Of those that a mesh axis runs over, the one named last changes fastest.
Arguments:
- hidden_in: bfloat16 [2, 8192, 1024], P(None, ('dp', 'expert')), may hold values from -6 to 6
- segment_ids: int32 [2, 8192], P(None, ('dp', 'expert')), may hold values from 0 to 64, as said below
- token_counts: int32 [2, 128], P(None, ('dp', 'expert')), may hold values from 32 to 64, as said below
- expert_ids: int32 [2, 8192, 8], P(None, ('dp', 'expert')), may hold values from 0 to 31, all different within a row; in each aligned block of 64 rows (0 to 63, 64 to 127, ..., all dimensions but the last counted through in order) at most 24 rows name the same one
- norm_one: bfloat16 [1024], P('dp'), may hold values from 0.5 to 1.5
- qkv_weight: bfloat16 [1024, 2048], P('dp'), may hold values from -0.1875 to 0.1875
- out_weight: bfloat16 [1024, 1024], P('dp'), may hold values from -0.75 to 0.75
- norm_two: bfloat16 [1024], P('dp'), may hold values from 0.5 to 1.5
- router_weight: bfloat16 [1024, 32], P('dp'), may hold values from -0.09375 to 0.09375
- gate_weight: bfloat16 [32, 1024, 512], P('expert'), may hold values from -0.1875 to 0.1875
- up_weight: bfloat16 [32, 1024, 512], P('expert'), may hold values from -0.1875 to 0.1875
- down_weight: bfloat16 [32, 512, 1024], P('expert'), may hold values from -1 to 1
- cotangent: bfloat16 [2, 8192, 1024], P(None, ('dp', 'expert')), may hold values from -6 to 6
Outputs:
- output: bfloat16 [2, 8192, 1024], P(None, ('dp', 'expert'))
- input_grad: float32 [2, 8192, 1024], P(None, ('dp', 'expert'))
- norm_one_grad: float32 [1024], P('dp')
- qkv_grad: float32 [1024, 2048], P('dp')
- out_proj_grad: float32 [1024, 1024], P('dp')
- norm_two_grad: float32 [1024], P('dp')
- router_grad: float32 [1024, 32], P('dp')
- gate_proj_grad: float32 [32, 1024, 512], P('expert')
- up_proj_grad: float32 [32, 1024, 512], P('expert')
- down_proj_grad: float32 [32, 512, 1024], P('expert')
Inputs may be any that keep to these rules, and one draw needn't show every extreme that they name: `expert_ids`: in each device's micro-batch (aligned blocks of 64 rows) no expert is named by more than 24 rows; a row names 8 different experts. `token_counts`: some device's micro-batch is full and some holds 32 live slots. `segment_ids`: within each device's micro-batch the ids never fall; slots from the token count on hold 64, live slots less.
All inputs are finite; a program needn't handle non-finite values.
Results may differ from a plain program's by a relative error of at most 0.023.
Values may be sent and summed in bfloat16 or wider, within the bound.
No kernel may reach another device: no remote copies, remote signals or barrier semaphores. Data moves between devices by JAX's collectives and lax.ppermute only.
A program may use at most 128 MiB of HBM per device.

v0:
```python
import functools

import jax
import jax.numpy as jnp
from jax import lax
from jax.experimental import pallas as pl
from jax.experimental.pallas import tpu as pltpu
from jax.sharding import Mesh
from jax.sharding import PartitionSpec as P

D = 1024
QUERY_HEADS = 16
KEY_VALUE_HEADS = 8
HEAD_SIZE = 64
FFE = 512
TOPK = 8
MICRO = 2
TOK_MB = 64
EXPERTS = 32
CAP = 24
ROWS = MICRO * TOK_MB
SLOTS = MICRO * CAP
EXTRA = 16
WIDE = ROWS + EXTRA
KV = KEY_VALUE_HEADS * HEAD_SIZE
SMALL_AT = D + D // 2
SHORT = pl.CostEstimate(flops=1_000_000, bytes_accessed=100_000, transcendentals=0)

epsilon = 1e-06
highest = lax.Precision.HIGHEST
f32 = jnp.float32
bf16 = jnp.bfloat16


def plane_pairs(first, second, swap):
    pairs = []
    for y in range(4):
        for z in range(4):
            for c in range(2):
                dy, dz = (first, second) if c == 0 else (second, first)
                target = (((y + dy) % 4) * 4 + (z + dz) % 4) * 2 + (c ^ swap)
                pairs.append(((y * 4 + z) * 2 + c, target))
    return pairs


def along_first(v, k):
    return lax.ppermute(v, ("y", "z", "core"), plane_pairs(k % 4, 0, 0))


def along_second(v, k):
    return lax.ppermute(v, ("y", "z", "core"), plane_pairs(0, k % 4, 0))


def swap_core(v):
    return lax.ppermute(v, "core", [(0, 1), (1, 0)])


def along_x(v, k):
    return lax.ppermute(v, "x", [(i, (i + k) % 4) for i in range(4)])


def stage(*values):
    return lax.optimization_barrier(values)


def spread_first(v):
    return [along_first(v, k) for k in (1, 2, 3)]


def add(first, *others):
    total = first.astype(f32)
    for v in others:
        total = total + v.astype(f32)
    return total


def nt(a, b):
    return lax.dot_general(a, b, (((1,), (1,)), ((), ())), preferred_element_type=f32)


def tn(a, b):
    return lax.dot_general(a, b, (((0,), (0,)), ((), ())), preferred_element_type=f32)


def nn(a, b):
    return jnp.dot(a, b, preferred_element_type=f32)


BLOCKS = 8
PACKED = BLOCKS * SLOTS


def expert_kernel(n_rows, n_grads, place_ref, *refs):
    row_refs, refs = refs[:n_rows], refs[n_rows:]
    grad_refs, refs = refs[:n_grads], refs[n_grads:]
    gate_ref, up_ref, down_ref = refs[:3]
    back_refs, out_refs, save_refs = refs[3:5], refs[5:7], refs[7:12]
    (row_buf, grad_buf, back_buf, out_buf, x_buf, c_buf, r_buf, s_buf, h_buf, g_buf, u_buf,
     mix_buf, pick_buf, dot_buf, gate_buf, up_buf, down_buf,
     row_sem, grad_sem, back_sem, out_sem, save_sem, weight_sem) = refs[12:]

    def pieces(sources, buf, sem):
        copies = []
        for ref in sources:
            for b in range(ref.shape[0]):
                at = len(copies)
                copies.append(pltpu.make_async_copy(ref.at[b], buf.at[at], sem.at[at]))
        return copies

    row_loads = pieces(row_refs, row_buf, row_sem)
    grad_loads = pieces(grad_refs, grad_buf, grad_sem)
    weight_loads = [
        pltpu.make_async_copy(ref, buf, weight_sem.at[i])
        for i, (ref, buf) in enumerate(
            zip((gate_ref, up_ref, down_ref), (gate_buf, up_buf, down_buf))
        )
    ]
    for one, two in zip(row_loads, grad_loads):
        one.start()
        two.start()
    for copy in weight_loads:
        copy.start()

    expert = place_ref[0]
    row_at = expert % 4
    lane_at = pl.multiple_of((expert // 4) * 128, 128)
    upper = (
        lax.broadcasted_iota(jnp.int32, (ROWS, ROWS), 0)
        < lax.broadcasted_iota(jnp.int32, (ROWS, ROWS), 1)
    ).astype(bf16)
    extra_row = lax.broadcasted_iota(jnp.int32, (EXTRA, 128), 0)
    slot_row = lax.broadcasted_iota(jnp.int32, (SLOTS, ROWS), 0).astype(f32)

    @pl.loop(0, BLOCKS)
    def _(b):
        pltpu.make_async_copy(row_refs[0].at[0], row_buf.at[b], row_sem.at[b]).wait()
        pltpu.make_async_copy(grad_refs[0].at[0], grad_buf.at[b], grad_sem.at[b]).wait()
        info = row_buf[b, ROWS:WIDE, pl.ds(lane_at, 128)].astype(f32)
        high = jnp.sum(jnp.where(extra_row == row_at, info, 0.0), axis=0, keepdims=True)
        low = jnp.sum(jnp.where(extra_row == row_at + 4, info, 0.0), axis=0, keepdims=True)
        chosen = high > 0.0
        flags = jnp.broadcast_to(chosen.astype(f32), (16, ROWS)).astype(bf16)
        rank = nn(flags, upper)[0:1]
        pick = jnp.where((slot_row == rank) & chosen, 1.0, 0.0)
        weight = jnp.sum(pick * (high + low), axis=1, keepdims=True)
        low_pick = pick.astype(bf16)
        pick_buf[b] = low_pick
        span = pl.ds(pl.multiple_of(b * SLOTS, SLOTS), SLOTS)
        mix_buf[span, :] = jnp.broadcast_to(weight, (SLOTS, 128))
        x_buf[span, :] = nn(low_pick, row_buf[b, 0:ROWS, :]).astype(bf16)
        c_buf[span, :] = nn(low_pick, grad_buf[b]).astype(bf16)

    saves = [
        pltpu.make_async_copy(buf, ref, save_sem.at[i])
        for i, (buf, ref) in enumerate(zip((x_buf, s_buf, h_buf, g_buf, u_buf), save_refs))
    ]
    saves[0].start()
    mixing = mix_buf[:, 0:1]
    grads = c_buf[...].astype(f32)
    s_buf[...] = (mixing * grads).astype(bf16)
    saves[1].start()
    for copy in weight_loads:
        copy.wait()
    gate_pre = nn(x_buf[...], gate_buf[...])
    up_pre = nn(x_buf[...], up_buf[...])
    sigma = 1.0 / (1.0 + jnp.exp(-gate_pre))
    swish = gate_pre * sigma
    h_buf[...] = (swish * up_pre).astype(bf16)
    saves[2].start()
    hidden_grad = nt(s_buf[...], down_buf[...])
    slope = sigma * (1.0 + gate_pre * (1.0 - sigma))
    g_buf[...] = (hidden_grad * up_pre * slope).astype(bf16)
    u_buf[...] = (hidden_grad * swish).astype(bf16)
    saves[3].start()
    saves[4].start()
    r_buf[...] = (nt(g_buf[...], gate_buf[...]) + nt(u_buf[...], up_buf[...])).astype(bf16)
    produced = nn(h_buf[...], down_buf[...]).astype(bf16).astype(f32)
    gate_grad = jnp.sum(produced * c_buf[...].astype(f32), axis=1, keepdims=True)
    dot_buf[...] = jnp.broadcast_to(gate_grad, (PACKED, 128))
    c_buf[...] = (mixing * produced).astype(bf16)

    @pl.loop(0, BLOCKS)
    def _(b):
        low_pick = pick_buf[b]
        span = pl.ds(pl.multiple_of(b * SLOTS, SLOTS), SLOTS)
        back_buf[b, 0:ROWS, :] = tn(low_pick, r_buf[span, :]).astype(bf16)
        out_buf[b] = tn(low_pick, c_buf[span, :]).astype(bf16)
        back_buf[b, ROWS:WIDE, :] = jnp.zeros((EXTRA, D), bf16)
        dots = jnp.sum(low_pick.astype(f32) * dot_buf[span, :], axis=0, keepdims=True)
        high = dots.astype(bf16).astype(f32)
        info = jnp.where(extra_row == row_at, high, 0.0)
        info = info + jnp.where(extra_row == row_at + 4, dots - high, 0.0)
        back_buf[b, ROWS:WIDE, pl.ds(lane_at, 128)] = info.astype(bf16)
        for side in range(2):
            @pl.when(b // 4 == side)
            def _():
                at = b - 4 * side
                pltpu.make_async_copy(back_buf.at[b], back_refs[side].at[at], back_sem.at[b]).start()
                pltpu.make_async_copy(out_buf.at[b], out_refs[side].at[at], out_sem.at[b]).start()

    for b in range(BLOCKS):
        side, at = b // 4, b % 4
        pltpu.make_async_copy(back_buf.at[b], back_refs[side].at[at], back_sem.at[b]).wait()
        pltpu.make_async_copy(out_buf.at[b], out_refs[side].at[at], out_sem.at[b]).wait()
    for copy in saves:
        copy.wait()


def run_experts(place, rows, grads, gate, up, down):
    any_space = pl.BlockSpec(memory_space=pl.ANY)
    wide = jax.ShapeDtypeStruct((4, WIDE, D), bf16)
    flat = jax.ShapeDtypeStruct((4, ROWS, D), bf16)
    full = jax.ShapeDtypeStruct((PACKED, D), bf16)
    half = jax.ShapeDtypeStruct((PACKED, FFE), bf16)
    return pl.pallas_call(
        functools.partial(expert_kernel, len(rows), len(grads)),
        in_specs=[pl.BlockSpec(memory_space=pltpu.SMEM)]
        + [any_space] * (len(rows) + len(grads) + 3),
        out_specs=[any_space] * 9,
        out_shape=[wide, wide, flat, flat, full, full, half, half, half],
        scratch_shapes=[
            pltpu.VMEM((BLOCKS, WIDE, D), bf16),
            pltpu.VMEM((BLOCKS, ROWS, D), bf16),
            pltpu.VMEM((BLOCKS, WIDE, D), bf16),
            pltpu.VMEM((BLOCKS, ROWS, D), bf16),
            pltpu.VMEM((PACKED, D), bf16),
            pltpu.VMEM((PACKED, D), bf16),
            pltpu.VMEM((PACKED, D), bf16),
            pltpu.VMEM((PACKED, D), bf16),
            pltpu.VMEM((PACKED, FFE), bf16),
            pltpu.VMEM((PACKED, FFE), bf16),
            pltpu.VMEM((PACKED, FFE), bf16),
            pltpu.VMEM((PACKED, 128), f32),
            pltpu.VMEM((BLOCKS, SLOTS, ROWS), bf16),
            pltpu.VMEM((PACKED, 128), f32),
            pltpu.VMEM((D, FFE), bf16),
            pltpu.VMEM((D, FFE), bf16),
            pltpu.VMEM((FFE, D), bf16),
            pltpu.SemaphoreType.DMA((BLOCKS,)),
            pltpu.SemaphoreType.DMA((BLOCKS,)),
            pltpu.SemaphoreType.DMA((BLOCKS,)),
            pltpu.SemaphoreType.DMA((BLOCKS,)),
            pltpu.SemaphoreType.DMA((5,)),
            pltpu.SemaphoreType.DMA((3,)),
        ],
        compiler_params=pltpu.CompilerParams(vmem_limit_bytes=60 * 1024 * 1024),
        cost_estimate=SHORT,
        name="experts",
    )(place, *rows, *grads, gate, up, down)


def weight_grad_kernel(*refs):
    xs, ss, hs, gs, us = (refs[4 * i:4 * i + 4] for i in range(5))
    out_ref = refs[20]
    x_buf, s_buf, h_buf, g_buf, u_buf, out_buf, in_sem, out_sem = refs[21:]
    loads = []
    for j in range(4):
        for i, (sources, buf) in enumerate(
            zip((xs, gs, us, hs, ss), (x_buf, g_buf, u_buf, h_buf, s_buf))
        ):
            loads.append(pltpu.make_async_copy(sources[j], buf.at[j], in_sem.at[j, i]))
    for copy in loads:
        copy.start()
    for copy in loads:
        copy.wait()

    @pl.loop(0, 4)
    def _(k):
        wide_at = pl.multiple_of(k * 256, 256)
        thin_at = pl.multiple_of(k * 128, 128)
        rows = x_buf[:, :, pl.ds(wide_at, 256)].reshape(4 * PACKED, 256)
        thin = h_buf[:, :, pl.ds(thin_at, 128)].reshape(4 * PACKED, 128)
        out_buf[k, 0:256, :] = tn(rows, g_buf[...].reshape(4 * PACKED, FFE)).astype(bf16)
        out_buf[k, 256:512, :] = tn(rows, u_buf[...].reshape(4 * PACKED, FFE)).astype(bf16)
        down = tn(thin, s_buf[...].reshape(4 * PACKED, D)).astype(bf16)
        out_buf[k, 512:640, :] = down[:, 0:FFE]
        out_buf[k, 640:768, :] = down[:, FFE:D]
        pltpu.make_async_copy(out_buf.at[k], out_ref.at[k], out_sem.at[k]).start()

    for k in range(4):
        pltpu.make_async_copy(out_buf.at[k], out_ref.at[k], out_sem.at[k]).wait()


def run_weight_grads(saved):
    operands = [part[i] for i in range(5) for part in saved]
    any_space = pl.BlockSpec(memory_space=pl.ANY)
    return pl.pallas_call(
        weight_grad_kernel,
        in_specs=[any_space] * 20,
        out_specs=any_space,
        out_shape=jax.ShapeDtypeStruct((4, 768, FFE), bf16),
        scratch_shapes=[
            pltpu.VMEM((4, PACKED, D), bf16),
            pltpu.VMEM((4, PACKED, D), bf16),
            pltpu.VMEM((4, PACKED, FFE), bf16),
            pltpu.VMEM((4, PACKED, FFE), bf16),
            pltpu.VMEM((4, PACKED, FFE), bf16),
            pltpu.VMEM((4, 768, FFE), bf16),
            pltpu.SemaphoreType.DMA((4, 5)),
            pltpu.SemaphoreType.DMA((4,)),
        ],
        compiler_params=pltpu.CompilerParams(vmem_limit_bytes=60 * 1024 * 1024),
        cost_estimate=SHORT,
        name="expert_weight_grads",
    )(*operands)


def blocks_behind(x_at, n):
    return [pl.multiple_of(((x_at + 4 - k) % 4) * n, n) for k in range(4)]


def swapped_halves(v):
    lane = lax.broadcasted_iota(jnp.int32, v.shape, 1)
    return jnp.where(lane % HEAD_SIZE < HEAD_SIZE // 2, pltpu.roll(v, 96, 1), pltpu.roll(v, 32, 1))


def pack_kernel(place_ref, qkv_ref, out_ref, router_ref, gains_ref, packed_ref, small_ref):
    core = place_ref[4]
    packed_ref[:, 0:D] = qkv_ref[:, pl.ds(pl.multiple_of(core * D, D), D)]
    packed_ref[:, D:SMALL_AT] = out_ref[:, pl.ds(pl.multiple_of(core * 512, 512), 512)]
    rows = [router_ref[...].astype(f32), gains_ref[...].astype(f32), jnp.zeros((94, 256), f32)]
    small = jnp.concatenate(rows, axis=0).T.astype(bf16)
    packed_ref[:, SMALL_AT:SMALL_AT + 128] = small
    small_ref[...] = small


def rest_copies(near_ref, far_ref, buf, sem, at, lane, width):
    columns = slice(lane, lane + width)
    return [
        pltpu.make_async_copy(near_ref.at[0:256, columns], buf.at[0:256], sem.at[at]),
        pltpu.make_async_copy(far_ref.at[:, columns], buf.at[256:512], sem.at[at + 1]),
        pltpu.make_async_copy(near_ref.at[256:512, columns], buf.at[512:768], sem.at[at + 2]),
    ]


def project_kernel(
    place_ref, x_ref, mine_ref, tiny_ref, table_ref, near_ref, far_ref, sib_near_ref, sib_far_ref,
    q_ref, kv_ref, small_ref,
    norm_buf, all_buf, tiny_buf, small_buf, own_buf, sib_buf, sem,
):
    x_at, core = place_ref[1], place_ref[4]
    lanes = blocks_behind(x_at, 256)
    small_loads = rest_copies(near_ref, far_ref, small_buf, sem, 0, SMALL_AT, 128)
    own_loads = rest_copies(near_ref, far_ref, own_buf, sem, 3, 0, D)
    sib_loads = rest_copies(sib_near_ref, sib_far_ref, sib_buf, sem, 6, 0, D)
    for copy in small_loads + own_loads + sib_loads:
        copy.start()
    for copy in small_loads:
        copy.wait()
    for k in range(4):
        piece = tiny_ref[...] if k == 0 else small_buf[(k - 1) * 256:k * 256, :]
        tiny_buf[:, pl.ds(lanes[k], 256)] = piece.astype(f32).T
    small_ref[...] = tiny_buf[0:40, :]
    x = x_ref[...].astype(f32)
    inverse = lax.rsqrt(jnp.mean(x * x, axis=1, keepdims=True) + epsilon)
    norm_buf[...] = (x * inverse * tiny_buf[32:33, :]).astype(bf16)
    rows = [norm_buf[:, pl.ds(at, 256)] for at in lanes]
    own_at = pl.multiple_of(core * D, D)
    sib_at = pl.multiple_of((1 - core) * D, D)
    for at, rest, loads in ((own_at, own_buf, own_loads), (sib_at, sib_buf, sib_loads)):
        total = nn(rows[0], mine_ref[:, pl.ds(at, D)])
        for copy in loads:
            copy.wait()
        for k in (1, 2, 3):
            total = total + nn(rows[k], rest[(k - 1) * 256:k * 256, :])
        all_buf[:, pl.ds(at, D)] = total
    cosine, sine = table_ref[:, 0:128], table_ref[:, 128:256]
    for c in range(12):
        v = all_buf[:, c * 128:(c + 1) * 128]
        turned = (v * cosine + swapped_halves(v) * sine).astype(bf16)
        if c < 8:
            q_ref[:, c * 128:(c + 1) * 128] = turned
        else:
            kv_ref[:, (c - 8) * 128:(c - 7) * 128] = turned
    kv_ref[:, KV:2 * KV] = all_buf[:, D + KV:D + 2 * KV].astype(bf16)


def head_scores(q_ref, kv_ref, allowed, h):
    chunk = q_ref[:, h * 128:(h + 1) * 128]
    query = jnp.concatenate([chunk[:, 0:64], chunk[:, 64:128]], axis=0)
    key = kv_ref[:, h * 64:(h + 1) * 64]
    value = kv_ref[:, KV + h * 64:KV + (h + 1) * 64]
    scores = jnp.where(allowed, nt(query, key) * HEAD_SIZE ** (-0.5), -1e30)
    expo = jnp.exp(scores - jnp.max(scores, axis=1, keepdims=True))
    probs = expo / jnp.sum(expo, axis=1, keepdims=True)
    return query, key, value, probs


def allowed_pairs(table_ref):
    shape = (2 * ROWS, ROWS)
    column = table_ref[:, 289:290]
    row = table_ref[:, 256:384].T[33:34]
    q = lax.broadcasted_iota(jnp.int32, shape, 0) % ROWS
    p = lax.broadcasted_iota(jnp.int32, shape, 1)
    return (jnp.concatenate([column, column], axis=0) == row) & (p <= q)


def attend_kernel(
    place_ref, x_ref, q_ref, kv_ref, small_ref, mine_ref, table_ref,
    near_ref, far_ref, sib_near_ref, sib_far_ref,
    line_ref, after_ref, gates_ref, sent_ref,
    low_buf, out_buf, own_buf, sib_buf, sem,
):
    x_at, core = place_ref[1], place_ref[4]
    loads = rest_copies(near_ref, far_ref, own_buf, sem, 0, D, 512)
    loads += rest_copies(sib_near_ref, sib_far_ref, sib_buf, sem, 3, D, 512)
    for copy in loads:
        copy.start()
    allowed = allowed_pairs(table_ref)
    for h in range(KEY_VALUE_HEADS):
        _, _, value, probs = head_scores(q_ref, kv_ref, allowed, h)
        got = nn(probs.astype(bf16), value)
        low_buf[:, h * 128:(h + 1) * 128] = jnp.concatenate(
            [got[0:ROWS], got[ROWS:2 * ROWS]], axis=1
        ).astype(bf16)
    rows = [low_buf[:, pl.ds(at, 256)] for at in blocks_behind(x_at, 256)]
    for k in range(4):
        line_ref[:, k * 256:(k + 1) * 256] = rows[k]
    own_at = pl.multiple_of(core * 512, 512)
    sib_at = pl.multiple_of((1 - core) * 512, 512)
    for copy in loads:
        copy.wait()
    for at, rest in ((own_at, own_buf), (sib_at, sib_buf)):
        total = nn(rows[0], mine_ref[:, pl.ds(at, 512)])
        for k in (1, 2, 3):
            total = total + nn(rows[k], rest[(k - 1) * 256:k * 256, :])
        out_buf[:, pl.ds(at, 512)] = total
    valid = table_ref[:, 288:289]
    after = x_ref[...].astype(f32) + valid * out_buf[...]
    after_ref[...] = after
    inverse = lax.rsqrt(jnp.mean(after * after, axis=1, keepdims=True) + epsilon)
    second = after * inverse * small_ref[33:34, :]
    logits = lax.dot_general(
        second, small_ref[0:32, :], (((1,), (1,)), ((), ())),
        precision=highest, preferred_element_type=f32,
    )
    member = table_ref[:, 256:288] > 0.0
    masked = jnp.where(member, logits, -3e38)
    gates = jnp.where(member, jnp.exp(masked - jnp.max(masked, axis=1, keepdims=True)), 0.0)
    gates = gates / jnp.sum(gates, axis=1, keepdims=True)
    gates_ref[...] = gates
    mixing = jnp.concatenate([gates * valid, jnp.zeros((ROWS, 96), f32)], axis=1).T
    high = mixing[0:32].astype(bf16).astype(f32)
    low = mixing[0:32] - high
    info = [
        jnp.concatenate([high[4 * q:4 * q + 4], low[4 * q:4 * q + 4], jnp.zeros((8, 128), f32)], axis=0)
        for q in range(8)
    ]
    sent_ref[0:ROWS, :] = second.astype(bf16)
    sent_ref[ROWS:WIDE, :] = jnp.concatenate(info, axis=1).astype(bf16)


def norm_backward(grad, values, gain):
    inverse = lax.rsqrt(jnp.mean(values * values, axis=1, keepdims=True) + epsilon)
    scaled = grad * gain
    gain_grad = jnp.sum(grad * values * inverse, axis=0, keepdims=True)
    dot = jnp.mean(scaled * values, axis=1, keepdims=True)
    return inverse * (scaled - values * (inverse * inverse * dot)), gain_grad


def attend_back_kernel(
    place_ref, b0, b1, b2, b3, cot_ref, after_ref, gates_ref, small_ref,
    mine_ref, q_ref, kv_ref, table_ref, near_ref, far_ref, sib_near_ref, sib_far_ref,
    mine_out, other_out, after_grad_ref, tiny_ref,
    low_buf, sum_buf, grad_buf, all_buf, own_buf, sib_buf, sem,
):
    x_at, first_at, second_at, core = (place_ref[i] for i in (1, 2, 3, 4))
    loads = rest_copies(near_ref, far_ref, own_buf, sem, 0, D, 512)
    loads += rest_copies(sib_near_ref, sib_far_ref, sib_buf, sem, 3, D, 512)
    for copy in loads:
        copy.start()
    back = b0[...].astype(f32) + b1[...].astype(f32) + b2[...].astype(f32) + b3[...].astype(f32)
    extra = back[ROWS:WIDE]
    dots = extra[0:4] + extra[4:8]
    dots = jnp.concatenate([dots[:, q * 128:(q + 1) * 128] for q in range(8)], axis=0)
    dots = jnp.concatenate([dots, jnp.zeros((96, ROWS), f32)], axis=0).T[:, 0:32]
    valid, gates = table_ref[:, 288:289], gates_ref[...]
    gate_grad = dots * valid
    logit_grad = gates * (gate_grad - jnp.sum(gates * gate_grad, axis=1, keepdims=True))
    after = after_ref[...]
    gain = small_ref[33:34, :]
    inverse = lax.rsqrt(jnp.mean(after * after, axis=1, keepdims=True) + epsilon)
    second = after * inverse * gain
    wide_grad = jnp.concatenate([logit_grad, jnp.zeros((ROWS, 96), f32)], axis=1)
    tiny_ref[0:32, :] = jnp.dot(
        wide_grad.T, second, precision=highest, preferred_element_type=f32
    )[0:32]
    second_grad = back[0:ROWS] + jnp.dot(
        logit_grad, small_ref[0:32, :], precision=highest, preferred_element_type=f32
    )
    norm_grad, gain_grad = norm_backward(second_grad, after, gain)
    tiny_ref[32:40, :] = jnp.concatenate(
        [jnp.zeros((1, D), f32), gain_grad, jnp.zeros((6, D), f32)], axis=0
    )
    after_grad = cot_ref[...].astype(f32) + norm_grad
    after_grad_ref[...] = after_grad
    low_buf[...] = (valid * after_grad).astype(bf16)
    own_at = pl.multiple_of(core * 512, 512)
    sib_at = pl.multiple_of((1 - core) * 512, 512)
    own = low_buf[:, pl.ds(own_at, 512)]
    other = low_buf[:, pl.ds(sib_at, 512)]
    for copy in loads:
        copy.wait()
    lanes = blocks_behind(x_at, 256)
    for k in range(4):
        if k == 0:
            got = nt(own, mine_ref[:, pl.ds(own_at, 512)]) + nt(other, mine_ref[:, pl.ds(sib_at, 512)])
        else:
            span = slice((k - 1) * 256, k * 256)
            got = nt(own, own_buf[span, :]) + nt(other, sib_buf[span, :])
        grad_buf[:, pl.ds(lanes[k], 256)] = got.astype(bf16)
    allowed = allowed_pairs(table_ref)
    cosine, sine = table_ref[:, 0:128], table_ref[:, 128:256]
    scale = HEAD_SIZE ** (-0.5)
    for h in range(KEY_VALUE_HEADS):
        query, key, value, probs = head_scores(q_ref, kv_ref, allowed, h)
        chunk = grad_buf[:, h * 128:(h + 1) * 128]
        grad = jnp.concatenate([chunk[:, 0:64], chunk[:, 64:128]], axis=0)
        prob_grad = nt(grad, value)
        score_grad = (
            probs * (prob_grad - jnp.sum(probs * prob_grad, axis=1, keepdims=True))
        ).astype(bf16)
        value_grad = tn(probs.astype(bf16), grad)
        query_grad = nn(score_grad, key) * scale
        key_grad = tn(score_grad, query) * scale
        sum_buf[:, h * 128:(h + 1) * 128] = jnp.concatenate(
            [query_grad[0:ROWS], query_grad[ROWS:2 * ROWS]], axis=1
        )
        sum_buf[:, D + h * 64:D + (h + 1) * 64] = key_grad
        all_buf[:, D + KV + h * 64:D + KV + (h + 1) * 64] = value_grad.astype(bf16)
    for c in range(12):
        v = sum_buf[:, c * 128:(c + 1) * 128]
        all_buf[:, c * 128:(c + 1) * 128] = (v * cosine - swapped_halves(v) * sine).astype(bf16)
    for f in range(4):
        at = (first_at + f) % 4
        mine_out[f, :, 0:256] = all_buf[:, pl.ds(pl.multiple_of(core * D + at * 256, 256), 256)]
        mine_out[f, :, 256:384] = low_buf[:, pl.ds(pl.multiple_of(core * 512 + at * 128, 128), 128)]
        at = (second_at + f) % 4
        other_out[f, :, 0:256] = all_buf[:, pl.ds(pl.multiple_of((1 - core) * D + at * 256, 256), 256)]
        other_out[f, :, 256:384] = low_buf[
            :, pl.ds(pl.multiple_of((1 - core) * 512 + at * 128, 128), 128)
        ]


def input_back_kernel(
    place_ref, mine_grad, other_grad, mine_ref, x_ref, after_grad_ref, small_ref, tiny_in,
    near_ref, far_ref, sib_near_ref, sib_far_ref,
    input_grad_ref, tiny_ref,
    own_buf, other_buf, grad_buf, own_rest, sib_rest, sem,
):
    x_at, first_at, second_at, core = (place_ref[i] for i in (1, 2, 3, 4))
    loads = rest_copies(near_ref, far_ref, own_rest, sem, 0, 0, D)
    loads += rest_copies(sib_near_ref, sib_far_ref, sib_rest, sem, 3, 0, D)
    for copy in loads:
        copy.start()
    for f in range(4):
        at = pl.multiple_of(((first_at + f) % 4) * 256, 256)
        own_buf[:, pl.ds(at, 256)] = mine_grad[f, :, 0:256]
        at = pl.multiple_of(((second_at + f) % 4) * 256, 256)
        other_buf[:, pl.ds(at, 256)] = other_grad[f, :, 0:256]
    own, other = own_buf[...], other_buf[...]
    own_at = pl.multiple_of(core * D, D)
    sib_at = pl.multiple_of((1 - core) * D, D)
    lanes = blocks_behind(x_at, 256)
    for copy in loads:
        copy.wait()
    for k in range(4):
        if k == 0:
            got = nt(own, mine_ref[:, pl.ds(own_at, D)]) + nt(other, mine_ref[:, pl.ds(sib_at, D)])
        else:
            span = slice((k - 1) * 256, k * 256)
            got = nt(own, own_rest[span, :]) + nt(other, sib_rest[span, :])
        grad_buf[:, pl.ds(lanes[k], 256)] = got
    norm_grad, gain_grad = norm_backward(
        grad_buf[...], x_ref[...].astype(f32), small_ref[32:33, :]
    )
    input_grad_ref[...] = after_grad_ref[...] + norm_grad
    tiny_ref[0:32, :] = tiny_in[0:32, :]
    tiny_ref[32:40, :] = jnp.concatenate([gain_grad, tiny_in[33:40, :]], axis=0)


def norm_line_kernel(place_ref, r0, r1, r2, r3, r4, r5, r6, r7, small_ref, out_ref):
    gain = small_ref[32:33, :]
    lanes = blocks_behind(place_ref[1], 256)
    for i, ref in enumerate((r0, r1, r2, r3, r4, r5, r6, r7)):
        x = ref[ref.shape[0] - ROWS:, :].astype(f32)
        inverse = lax.rsqrt(jnp.mean(x * x, axis=1, keepdims=True) + epsilon)
        out_ref[i * ROWS:(i + 1) * ROWS, :] = (x * inverse * gain).astype(bf16)
    pieces = [out_ref[:, pl.ds(lane, 256)] for lane in lanes]
    for k in range(4):
        out_ref[:, k * 256:(k + 1) * 256] = pieces[k]


def attention_weights_kernel(
    place_ref, n_ref, a0, a1, a2, a3, g0, g1, g2, g3, g4, tiny_ref,
    o0, o1, o2, o3,
    sum_buf, tiny_buf,
):
    x_at = place_ref[1]
    grads = [jnp.concatenate([g0[0], g1[0]], axis=0), g2[...], g3[...], g4[...]]
    out_sum = in_sum = None
    at = 0
    for ref, grad in zip((a0, a1, a2, a3), grads):
        one = tn(ref[...], grad[:, 256:384])
        two = tn(n_ref[at:at + ref.shape[0], :], grad[:, 0:256])
        out_sum = one if out_sum is None else out_sum + one
        in_sum = two if in_sum is None else in_sum + two
        at += ref.shape[0]
    sum_buf[:, 0:256] = in_sum
    sum_buf[:, 256:384] = out_sum
    tiny_buf[0:40, :] = tiny_ref[...]
    tiny_buf[40:128, :] = jnp.zeros((88, D), f32)
    for k, lane in enumerate(blocks_behind(x_at, 256)):
        sum_buf[k * 256:(k + 1) * 256, 384:512] = tiny_buf[:, pl.ds(lane, 256)].T
    for k, out in enumerate((o0, o1, o2, o3)):
        out[...] = sum_buf[k * 256:(k + 1) * 256, :].astype(bf16)


def collect_kernel(place_ref, p0, p1, p2, p3, out_ref):
    tiny = None
    for ref, wide, thin in zip(
        (p0, p1, p2, p3), blocks_behind(place_ref[2], 256), blocks_behind(place_ref[2], 128)
    ):
        out_ref[:, pl.ds(wide, 256)] = ref[:, 0:256]
        out_ref[:, pl.ds(pl.multiple_of(D + thin, 128), 128)] = ref[:, 256:384]
        one = ref[:, 384:512].astype(f32)
        tiny = one if tiny is None else tiny + one
    out_ref[:, SMALL_AT:SMALL_AT + 128] = tiny.astype(bf16)


def finish_kernel(place_ref, own_ref, other_ref, qkv_ref, out_ref, router_ref, one_ref, two_ref):
    core = place_ref[4]
    for ref, side in ((own_ref, core), (other_ref, 1 - core)):
        qkv_ref[:, pl.ds(pl.multiple_of(side * D, D), D)] = ref[:, 0:D].astype(f32)
        out_ref[:, pl.ds(pl.multiple_of(side * 512, 512), 512)] = ref[:, D:SMALL_AT].astype(f32)
    tiny = own_ref[:, SMALL_AT:SMALL_AT + 128].astype(f32)
    tiny = tiny + other_ref[:, SMALL_AT:SMALL_AT + 128].astype(f32)
    router_ref[...] = tiny[:, 0:EXPERTS]
    turned = tiny.T
    one_ref[...] = turned[32:33]
    two_ref[...] = turned[33:34]


def widen_kernel(sum_ref, gate_ref, up_ref, down_ref):
    gate_ref[...] = sum_ref[0, 0:256, :].astype(f32)
    up_ref[...] = sum_ref[0, 256:512, :].astype(f32)
    down_ref[:, 0:FFE] = sum_ref[0, 512:640, :].astype(f32)
    down_ref[:, FFE:D] = sum_ref[0, 640:768, :].astype(f32)


def widen(sums):
    return pl.pallas_call(
        widen_kernel,
        grid=(4,),
        in_specs=[pl.BlockSpec((1, 768, FFE), lambda k: (k, 0, 0))],
        out_specs=[
            pl.BlockSpec((256, FFE), lambda k: (k, 0)),
            pl.BlockSpec((256, FFE), lambda k: (k, 0)),
            pl.BlockSpec((128, D), lambda k: (k, 0)),
        ],
        out_shape=[
            jax.ShapeDtypeStruct((D, FFE), f32),
            jax.ShapeDtypeStruct((D, FFE), f32),
            jax.ShapeDtypeStruct((FFE, D), f32),
        ],
        compiler_params=pltpu.CompilerParams(vmem_limit_bytes=60 * 1024 * 1024),
        cost_estimate=SHORT,
        name="widen",
    )(sums)


def run_local(kernel, name, place, operands, outs, scratch, fetched=(), room=60):
    vmem = pl.BlockSpec(memory_space=pltpu.VMEM)
    apart = pl.BlockSpec(memory_space=pl.ANY)
    return pl.pallas_call(
        kernel,
        in_specs=[pl.BlockSpec(memory_space=pltpu.SMEM)]
        + [vmem] * len(operands)
        + [apart] * len(fetched),
        out_specs=[vmem] * len(outs),
        out_shape=[jax.ShapeDtypeStruct(shape, kind) for shape, kind in outs],
        scratch_shapes=[pltpu.VMEM(shape, kind) for shape, kind in scratch]
        + ([pltpu.SemaphoreType.DMA((9,))] if fetched else []),
        compiler_params=pltpu.CompilerParams(vmem_limit_bytes=room * 1024 * 1024),
        cost_estimate=SHORT,
        name=name,
    )(place, *operands, *fetched)


def block_at(v, index, size, axis):
    return lax.dynamic_slice_in_dim(v, index * size, size, axis)


def per_device(
    hidden_in,
    segment_ids,
    token_counts,
    expert_ids,
    norm_one,
    qkv_weight,
    out_weight,
    norm_two,
    router_weight,
    gate_weight,
    up_weight,
    down_weight,
    cotangent,
):
    x_at = lax.axis_index("x")
    y_at = lax.axis_index("y")
    z_at = lax.axis_index("z")
    core = lax.axis_index("core")
    first_at = jnp.where(core == 0, y_at, z_at)
    second_at = jnp.where(core == 0, z_at, y_at)
    place = jnp.stack([(y_at * 4 + z_at) * 2 + core, x_at, first_at, second_at, core]).astype(jnp.int32)

    grad_low = cotangent.reshape(ROWS, D)
    inputs = hidden_in.reshape(ROWS, D)
    valid = (
        (jnp.arange(TOK_MB, dtype=jnp.int32)[None, :] < token_counts).reshape(ROWS, 1).astype(f32)
    )
    segment_key = (
        segment_ids + (TOK_MB + 1) * jnp.arange(MICRO, dtype=jnp.int32)[:, None]
    ).reshape(ROWS)
    column, row = segment_key[:, None], segment_key[None, :]
    places = jnp.arange(ROWS)
    allowed = (column == row) & (places[:, None] >= places[None, :])
    position = jnp.sum(allowed.astype(f32), axis=1) - 1.0
    frequency = 10000.0 ** (-2.0 * jnp.arange(HEAD_SIZE // 2, dtype=f32) / HEAD_SIZE)
    angles = position[:, None] * frequency[None, :]
    cosine, sine = jnp.cos(angles), jnp.sin(angles)
    routes = expert_ids.reshape(ROWS, TOPK)
    member = jnp.any(
        routes[:, :, None] == jnp.arange(EXPERTS, dtype=jnp.int32)[None, None, :], axis=1
    ).astype(f32)
    table = jnp.concatenate(
        [cosine] * 4 + [-sine, sine, -sine, sine]
        + [member, valid, column.astype(f32), jnp.zeros((ROWS, 94), f32)],
        axis=1,
    )

    packed, small = run_local(
        pack_kernel, "pack", place,
        [qkv_weight, out_weight, router_weight.T, jnp.stack([norm_one, norm_two])],
        [((256, SMALL_AT + 128), bf16), ((256, 128), bf16)],
        [],
    )
    rows_pack = jnp.concatenate([grad_low, inputs], axis=0)
    from_back, from_ahead = along_x(packed, 1), along_x(packed, -1)
    rows_pack, _, inputs_sib = stage(rows_pack, packed, swap_core(inputs))
    lines_pack = spread_first(rows_pack)
    grad_rows = jnp.stack([grad_low] + [v[:ROWS] for v in lines_pack])
    first_values = swap_core(from_back[:16, SMALL_AT:])
    back, ahead, lines_pack, grad_rows, table, _ = stage(
        from_back, from_ahead, lines_pack, grad_rows, table, first_values
    )
    own_near = jnp.concatenate([back, ahead], axis=0)
    low, high, grad_back, grad_ahead, sib_near = stage(
        along_x(back[:128], 1), along_x(ahead[128:], -1),
        along_second(grad_rows, 1), along_second(grad_rows, -1), swap_core(own_near),
    )
    own_far = jnp.concatenate([low, high], axis=0)
    fetched = [own_near, own_far, sib_near, swap_core(own_far)]
    half = (ROWS, D)
    rest = ((768, 512), bf16)
    rest_wide = ((768, D), bf16)
    query, kv, small_full = run_local(
        project_kernel, "project", place,
        [inputs, qkv_weight, small, table],
        [(half, bf16), (half, bf16), ((40, D), f32)],
        [(half, bf16), ((ROWS, 2 * D), f32), ((128, D), f32), ((768, 128), bf16), rest_wide, rest_wide],
        fetched,
    )
    attended = run_local(
        attend_kernel, "attend", place,
        [inputs, query, kv, small_full, out_weight, table],
        [(half, bf16), (half, f32), ((ROWS, EXPERTS), f32), ((WIDE, D), bf16)],
        [(half, bf16), (half, f32), rest, rest],
        fetched,
    )
    attended, grad_two, sib_lines = stage(
        attended, along_second(grad_rows, 2), spread_first(inputs_sib)
    )
    line, after, gates, sent = attended

    def visit(rows, grads):
        return run_experts(place, rows, grads, gate_weight[0], up_weight[0], down_weight[0])

    pair = jnp.concatenate([line, swap_core(line)], axis=0)
    got, pair, rows_sib = stage(spread_first(sent), pair, swap_core(grad_rows))
    rows = jnp.stack([sent] + got)
    parts = {}
    parts[0], back, ahead, grad_two_sib, rows = stage(
        visit([rows, swap_core(rows)], [grad_rows, rows_sib]),
        along_second(rows, 1), along_second(rows, -1), swap_core(grad_two), rows,
    )
    parts[1], two, back_sib, ahead_sib, grad_back_sib, grad_ahead_sib = stage(
        visit([back, ahead], [grad_back, grad_ahead]), along_second(rows, 2),
        swap_core(back), swap_core(ahead), swap_core(grad_back), swap_core(grad_ahead),
    )
    parts[3], two_sib, lines = stage(
        visit([back_sib, ahead_sib], [grad_back_sib, grad_ahead_sib]),
        swap_core(two), spread_first(pair),
    )
    normed_line, = run_local(
        norm_line_kernel, "norm_line", place,
        [inputs, inputs_sib, lines_pack[0], sib_lines[0], lines_pack[1], sib_lines[1],
         lines_pack[2], sib_lines[2], small_full], [((8 * ROWS, D), bf16)], [],
    )
    normed_line, turn_back, turn_ahead = stage(
        normed_line, swap_core(parts[3][0]), swap_core(parts[3][1])
    )
    merged_back = add(parts[1][0], turn_back).astype(bf16)
    merged_ahead = add(parts[1][1], turn_ahead).astype(bf16)
    parts[2], got_back, got_ahead, turn_own = stage(
        visit([two, two_sib], [grad_two, grad_two_sib]), along_second(merged_back, -1), along_second(merged_ahead, -3),
        swap_core(parts[0][1]),
    )
    merged = add(parts[2][0], swap_core(parts[2][1])).astype(bf16)
    saved = [parts[j][4:9] for j in range(4)]
    merged, first_rows = stage(merged, saved[0][0])
    saved[0] = [first_rows] + list(saved[0][1:])
    partial = add(parts[0][0], turn_own, got_back, got_ahead).astype(bf16)
    chunks, partial, got_two, turn_back, turn_ahead, turn_two = stage(
        run_weight_grads(saved), partial, along_second(merged, -2),
        swap_core(parts[3][2]), swap_core(parts[3][3]), swap_core(parts[2][3]),
    )
    owned = lax.psum_scatter(chunks.reshape(4 * 768, FFE), "x", scatter_dimension=0, tiled=True)
    total = add(partial, got_two).astype(bf16)
    total, turn_back, turn_ahead, turn_two = stage(total, turn_back, turn_ahead, turn_two)
    merged_back = add(parts[1][2], turn_back).astype(bf16)
    merged_ahead = add(parts[1][3], turn_ahead).astype(bf16)
    merged = add(parts[2][2], turn_two).astype(bf16)
    arrived, merged_back, merged_ahead, merged, turn_own = stage(
        [along_first(total[i], -i) for i in (1, 2, 3)], merged_back, merged_ahead, merged,
        swap_core(parts[0][3]),
    )
    back = [total[0]] + arrived
    mine_grad, other_grad, after_grad, tiny = run_local(
        attend_back_kernel, "attend_back", place,
        back + [
            grad_low, after, gates, small_full, out_weight, query, kv, table,
        ],
        [((4, ROWS, 384), bf16), ((4, ROWS, 384), bf16), (half, f32), ((40, D), f32)],
        [(half, bf16), ((ROWS, 3 * KV), f32), (half, bf16), ((ROWS, 2 * D), bf16), rest, rest],
        fetched,
    )
    mine_grad, other_grad, sib_grad, got_back, got_ahead = stage(
        mine_grad, other_grad, swap_core(other_grad),
        along_second(merged_back, -1), along_second(merged_ahead, -3),
    )
    input_grad, tiny = run_local(
        input_back_kernel, "input_back", place,
        [mine_grad, other_grad, qkv_weight, inputs, after_grad, small_full, tiny],
        [(half, f32), ((40, D), f32)],
        [(half, bf16), (half, bf16), (half, f32), rest_wide, rest_wide],
        fetched,
    )
    line_grad = [
        along_first(jnp.concatenate([mine_grad[k], sib_grad[k]], axis=0), k) for k in (1, 2, 3)
    ]
    line_grad, input_grad, tiny, owned = stage(line_grad, input_grad, tiny, owned)
    expert_sums = lax.all_gather(owned, "x", axis=0, tiled=True)
    chunk = run_local(
        attention_weights_kernel, "attention_weights", place,
        [normed_line, pair, *lines, mine_grad, sib_grad, *line_grad, tiny],
        [((256, 512), bf16)] * 4,
        [((D, 512), f32), ((128, D), f32)],
    )
    chunk, got, got_two = stage(
        chunk, [along_x(chunk[k], -k) for k in (1, 2, 3)], along_second(merged, -2)
    )
    shard = add(chunk[0], *got).astype(bf16)
    total = add(parts[0][2], turn_own, got_back, got_ahead, got_two).astype(bf16)
    shard, got, total, arrived, expert_sums = stage(
        shard, [along_second(shard, k) for k in (1, 2, 3)],
        total, [along_first(total[i], -i) for i in (1, 3)], expert_sums,
    )
    shard = add(shard, *got).astype(bf16)
    gate_total, up_total, down_total = widen(expert_sums.reshape(4, 768, FFE))
    shard, got, gate_total, up_total, down_total, arrived_two = stage(
        shard, spread_first(shard), gate_total, up_total, down_total, along_first(total[2], -2)
    )
    output = (after + add(total[0], *arrived, arrived_two)).astype(bf16).reshape(MICRO, TOK_MB, D)
    both, = run_local(
        collect_kernel, "collect", place, [shard, *got], [((256, SMALL_AT + 128), bf16)], []
    )
    qkv_grad, out_grad, router_grad, gain_one, gain_two = run_local(
        finish_kernel, "finish", place, [both, swap_core(both)],
        [
            ((256, 2 * D), f32), ((256, D), f32), ((256, EXPERTS), f32),
            ((1, 256), f32), ((1, 256), f32),
        ],
        [],
    )

    return (
        output,
        input_grad.reshape(MICRO, TOK_MB, D),
        gain_one.reshape(256),
        qkv_grad,
        out_grad,
        gain_two.reshape(256),
        router_grad,
        gate_total[None],
        up_total[None],
        down_total[None],
    )


def solution(mesh):
    grid = Mesh(mesh.devices.reshape(4, 4, 4, 2), ("x", "y", "z", "core"))
    every = ("x", "y", "z", "core")
    plane = ("y", "z", "core")
    return jax.shard_map(
        per_device,
        mesh=grid,
        in_specs=(
            P(None, every, None),
            P(None, every),
            P(None, every),
            P(None, every, None),
            P("x"),
            P("x", None),
            P("x", None),
            P("x"),
            P("x", None),
            P(plane, None, None),
            P(plane, None, None),
            P(plane, None, None),
            P(None, every, None),
        ),
        out_specs=(
            P(None, every, None),
            P(None, every, None),
            P("x"),
            P("x", None),
            P("x", None),
            P("x"),
            P("x", None),
            P(plane, None, None),
            P(plane, None, None),
            P(plane, None, None),
        ),
        check_vma=False,
    )
```

profile of v0, /device:TPU:1, one launch (start us, length us, event | category | flops | bytes accessed | tf_op | source)
XLA Modules:
  0.0 323.2 jit_solution(17553873952245638803)
XLA Ops:
  12.3 3.3 %collective-permute-start.1 = (bf16[256,1664]{1,0:T(8,128)(2,1)}, bf16[256,1664]{1,0:T(8,128)(2,1)S(1)}, u32[]{:S(2)}, u32[]{:S(2)}) collective-permute-start(bf16[256,1664]{1,0:T(8,128)(2,1)} %get-tuple-element.207), channel_id=1, source_target_pairs={{0,96},{32,0},{64,32},{96,64},{1,97},{33,1},{65,33},{97,65},{2,98}... | collective-permute-start | bytes 2555912 | tf_op jit(solution)/shard_map/ppermute | solution.py:59
  17.9 3.8 %collective-permute-start.5 = (bf16[256,1024]{1,0:T(8,128)(2,1)}, bf16[256,1024]{1,0:T(8,128)(2,1)S(1)}, u32[]{:S(2)}, u32[]{:S(2)}) collective-permute-start(bf16[256,1024]{1,0:T(8,128)(2,1)} %pad_maximum_fusion.2), channel_id=1, source_target_pairs={{0,24},{1,7},{2,26},{3,1},{4,28},{5,3},{6,30},{7,5},{8,0},{9,15},{... | collective-permute-start | bytes 1572872 | tf_op jit(solution)/shard_map/ppermute | solution.py:47
  24.1 9.6 %collective-permute-done.5.r6 = bf16[256,1024]{1,0:T(8,128)(2,1)S(1)} collective-permute-done((bf16[256,1024]{1,0:T(8,128)(2,1)}, bf16[256,1024]{1,0:T(8,128)(2,1)S(1)}, u32[]{:S(2)}, u32[]{:S(2)}) %collective-permute-start.5) | collective-permute-done | bytes 524320 | tf_op jit(solution)/shard_map/ppermute | solution.py:47
  33.8 3.8 %collective-permute-done.3.r2 = bf16[256,1024]{1,0:T(8,128)(2,1)} collective-permute-done((bf16[256,1024]{1,0:T(8,128)(2,1)}, bf16[256,1024]{1,0:T(8,128)(2,1)}, u32[]{:S(2)}, u32[]{:S(2)}) %collective-permute-start.3) | collective-permute-done | bytes 524320 | tf_op jit(solution)/shard_map/ppermute | solution.py:47
  45.6 6.9 %collective-permute-done.7 = bf16[128,1664]{1,0:T(8,128)(2,1)S(1)} collective-permute-done((bf16[128,1664]{1,0:T(8,128)(2,1)S(1)}, bf16[128,1664]{1,0:T(8,128)(2,1)S(1)}, u32[]{:S(2)}, u32[]{:S(2)}) %collective-permute-start.7) | collective-permute-done | bytes 426016 | tf_op jit(solution)/shard_map/ppermute | solution.py:59
  68.1 5.1 %project.1 = (bf16[128,1024]{1,0:T(8,128)(2,1)}, bf16[128,1024]{1,0:T(8,128)(2,1)}, f32[40,1024]{1,0:T(8,128)}) custom-call(s32[5]{0:T(128)} %stack.59.place_ref, bf16[128,1024]{1,0:T(8,128)(2,1)} %bitcast.76, bf16[256,2048]{1,0:T(8,128)(2,1)} %mine_ref.7, bf16[256,128]{1,0:T(8,128)(2,1)} %get-tuple-element.206.tiny_ref, f32[128,384]{1,0:T(8,128)} %concatenate.25.table_ref, ...), custom_call_target="tpu_custom_call" | custom-call | flops 1000000 | bytes 100000 | tf_op jit(solution)/shard_map/project/pallas_call | solution.py:675
  73.2 6.8 %attend.1 = (bf16[128,1024]{1,0:T(8,128)(2,1)}, f32[128,1024]{1,0:T(8,128)}, f32[128,32]{1,0:T(8,128)}, bf16[144,1024]{1,0:T(8,128)(2,1)}) custom-call(s32[5]{0:T(128)} %stack.59.place_ref, bf16[128,1024]{1,0:T(8,128)(2,1)} %bitcast.77, bf16[128,1024]{1,0:T(8,128)(2,1)} %get-tuple-element.216.q_ref, bf16[128,1024]{1,0:T(8,128)(2,1)} %get-tuple-element.217.kv_ref, ...), custom_call_target="tpu_custom_call" | custom-call | flops 1000000 | bytes 100000 | tf_op jit(solution)/shard_map/attend/pallas_call | solution.py:675
  80.9 3.5 %collective-permute-done.12.refs_2_ = bf16[4,128,1024]{2,1,0:T(8,128)(2,1)S(1)} collective-permute-done((bf16[4,128,1024]{2,1,0:T(8,128)(2,1)}, bf16[4,128,1024]{2,1,0:T(8,128)(2,1)S(1)}, u32[]{:S(2)}, u32[]{:S(2)}) %collective-permute-start.12) | collective-permute-done | bytes 1048608 | tf_op jit(solution)/shard_map/ppermute | solution.py:51
  101.9 11.2 %experts.4 = (bf16[4,144,1024]{2,1,0:T(8,128)(2,1)}, bf16[4,144,1024]{2,1,0:T(8,128)(2,1)}, bf16[4,128,1024]{2,1,0:T(8,128)(2,1)}, bf16[4,128,1024]{2,1,0:T(8,12...) custom-call(s32[5]{0:T(128)} %stack.59.place_ref, ...), custom_call_target="tpu_custom_call" | custom-call | flops 1000000 | bytes 100000 | tf_op jit(solution)/shard_map/experts/pallas_call | solution.py:215
  119.1 11.3 %experts.5 = (bf16[4,144,1024]{2,1,0:T(8,128)(2,1)}, bf16[4,144,1024]{2,1,0:T(8,128)(2,1)}, bf16[4,128,1024]{2,1,0:T(8,128)(2,1)}, bf16[4,128,1024]{2,1,0:T(8,12...) custom-call(s32[5]{0:T(128)} %stack.59.place_ref, ...), custom_call_target="tpu_custom_call" | custom-call | flops 1000000 | bytes 100000 | tf_op jit(solution)/shard_map/experts/pallas_call | solution.py:215
  132.6 3.9 %collective-permute-start.30 = (bf16[4,144,1024]{2,1,0:T(8,128)(2,1)S(1)}, bf16[4,144,1024]{2,1,0:T(8,128)(2,1)S(1)}, u32[]{:S(2)}, u32[]{:S(2)}) collective-permute-start(bf16[4,144,1024]{2,1,0:T(8,128)(2,1)S(1)} %collective-permute-done.25.refs_0_), channel_id=1, source_target_pairs={{0,1},{1,0},{2,3},{3,2},{4,5},{5,4},{6,7},{7,6},{8,9},{9,8},{10,11... | collective-permute-start | bytes 3538952 | tf_op jit(solution)/shard_map/ppermute | solution.py:55
  137.9 11.3 %experts.6 = (bf16[4,144,1024]{2,1,0:T(8,128)(2,1)}, bf16[4,144,1024]{2,1,0:T(8,128)(2,1)}, bf16[4,128,1024]{2,1,0:T(8,128)(2,1)}, bf16[4,128,1024]{2,1,0:T(8,12...) custom-call(s32[5]{0:T(128)} %stack.59.place_ref, ...), custom_call_target="tpu_custom_call" | custom-call | flops 1000000 | bytes 100000 | tf_op jit(solution)/shard_map/experts/pallas_call | solution.py:215
  154.6 4.5 %norm_line.1.n_ref = bf16[1024,1024]{1,0:T(8,128)(2,1)} custom-call(s32[5]{0:T(128)} %stack.59.place_ref, bf16[128,1024]{1,0:T(8,128)(2,1)} %bitcast.78, bf16[128,1024]{1,0:T(8,128)(2,1)} %collective-permute-done.2.r1, bf16[256,1024]{1,0:T(8,128)(2,1)} %collective-permute-done.3.r2, bf16[128,1024]{1,0:T(8,128)(2,1)} %collective-permute-done.13.r3, ...), custom_call_target="tpu_custom_call" | custom-call | flops 1000000 | bytes 100000 | tf_op jit(solution)/shard_map/norm_line/pallas_call | solution.py:675
  163.8 11.2 %experts.7 = (bf16[4,144,1024]{2,1,0:T(8,128)(2,1)}, bf16[4,144,1024]{2,1,0:T(8,128)(2,1)}, bf16[4,128,1024]{2,1,0:T(8,128)(2,1)}, bf16[4,128,1024]{2,1,0:T(8,12...) custom-call(s32[5]{0:T(128)} %stack.59.place_ref, ...), custom_call_target="tpu_custom_call" | custom-call | flops 1000000 | bytes 100000 | tf_op jit(solution)/shard_map/experts/pallas_call | solution.py:215
  188.9 11.0 %expert_weight_grads.1 = bf16[4,768,512]{2,1,0:T(8,128)(2,1)} custom-call(bf16[384,1024]{1,0:T(8,128)(2,1)} %get-tuple-element.301.refs_0_, bf16[384,1024]{1,0:T(8,128)(2,1)} %get-tuple-element.302.refs_1_, bf16[384,1024]{1,0:T(8,128)(2,1)} %get-tuple-element.303.refs_2_, bf16[384,1024]{1,0:T(8,128)(2,1)} %get-tuple-element.304.refs_3_, ...), custom_call_target="tpu_custom_call" | custom-call | flops 1000000 | bytes 100000 | tf_op jit(solution)/shard_map/expert_weight_grads/pallas_call | solution.py:287
  206.9 3.8 %add_convert_fusion.7 = (bf16[4,128,1024]{2,1,0:T(8,128)(2,1)}, bf16[4,128,1024]{2,1,0:T(8,128)(2,1)}) fusion(bf16[4,128,1024]{2,1,0:T(8,128)(2,1)} %collective-permute-done.42, bf16[4,128,1024]{2,1,0:T(8,128)(2,1)S(1)} %copy-done.26, bf16[4,128,1024]{2,1,0:T(8,128)(2,1)} %collective-permute-done.41, bf16[4,128,1024]{2,1,0:T(8,128)(2,1)S(1)} %copy-done.25), kind=kLoop, calls=%fused_computation.7 | loop fusion | flops 4194304 | bytes 6291456 | tf_op jit(solution)/shard_map/convert_element_type | solution.py:832
  216.6 9.7 %attend_back.1 = (bf16[4,128,384]{2,1,0:T(8,128)(2,1)}, bf16[4,128,384]{2,1,0:T(8,128)(2,1)}, f32[128,1024]{1,0:T(8,128)}, f32[40,1024]{1,0:T(8,128)}) custom-call(s32[5]{0:T(128)} %stack.59.place_ref, bf16[144,1024]{1,0:T(8,128)(2,1)} %get-tuple-element.447.b0, bf16[144,1024]{1,0:T(8,128)(2,1)} %copy-done.34, bf16[144,1024]{1,0:T(8,128)(2,1)} %copy-done.32, ...), custom_call_target="tpu_custom_call" | custom-call | flops 1000000 | bytes 100000 | tf_op jit(solution)/shard_map/attend_back/pallas_call | solution.py:675
  232.4 3.4 %collective-permute-start.52 = (bf16[256,384]{1,0:T(8,128)(2,1)S(1)}, bf16[256,384]{1,0:T(8,128)(2,1)S(1)}, u32[]{:S(2)}, u32[]{:S(2)}) collective-permute-start(bf16[256,384]{1,0:T(8,128)(2,1)S(1)} %pad_maximum_fusion.5), channel_id=1, source_target_pairs={{0,16},{1,5},{2,18},{3,7},{4,20},{5,1},{6,22},{7,3},{8,24},{9,13},... | collective-permute-start | bytes 589832 | tf_op jit(solution)/shard_map/ppermute | solution.py:47
  235.8 6.2 %input_back.1 = (f32[128,1024]{1,0:T(8,128)}, f32[40,1024]{1,0:T(8,128)}) custom-call(s32[5]{0:T(128)} %stack.59.place_ref, bf16[4,128,384]{2,1,0:T(8,128)(2,1)} %get-tuple-element.350.mine_grad.g0, bf16[4,128,384]{2,1,0:T(8,128)(2,1)} %get-tuple-element.352.other_grad, bf16[256,2048]{1,0:T(8,128)(2,1)} %mine_ref.7, bf16[128,1024]{1,0:T(8,128)(2,1)} %bitcast.79, ...), custom_call_target="tpu_custom_call" | custom-call | flops 1000000 | bytes 100000 | tf_op jit(solution)/shard_map/input_back/pallas_call | solution.py:675
  242.9 4.9 %attention_weights.1 = (bf16[256,512]{1,0:T(8,128)(2,1)}, bf16[256,512]{1,0:T(8,128)(2,1)}, bf16[256,512]{1,0:T(8,128)(2,1)}, bf16[256,512]{1,0:T(8,128)(2,1)}) custom-call(s32[5]{0:T(128)} %stack.59.place_ref, bf16[1024,1024]{1,0:T(8,128)(2,1)} %norm_line.1.n_ref, bf16[256,1024]{1,0:T(8,128)(2,1)} %copy-done.8, ...), custom_call_target="tpu_custom_call" | custom-call | flops 1000000 | bytes 100000 | tf_op jit(solution)/shard_map/attention_weights/pallas_call | solution.py:675
  249.2 8.6 %collective-permute-done.57 = bf16[4,128,1024]{2,1,0:T(8,128)(2,1)} collective-permute-done((bf16[4,128,1024]{2,1,0:T(8,128)(2,1)S(1)}, bf16[4,128,1024]{2,1,0:T(8,128)(2,1)}, u32[]{:S(2)}, u32[]{:S(2)}) %collective-permute-start.57) | collective-permute-done | bytes 1048608 | tf_op jit(solution)/shard_map/ppermute | solution.py:51
  257.8 10.7 %collective-permute-done.56 = bf16[256,512]{1,0:T(8,128)(2,1)S(1)} collective-permute-done((bf16[256,512]{1,0:T(8,128)(2,1)}, bf16[256,512]{1,0:T(8,128)(2,1)S(1)}, u32[]{:S(2)}, u32[]{:S(2)}) %collective-permute-start.56) | collective-permute-done | bytes 262176 | tf_op jit(solution)/shard_map/ppermute | solution.py:59
  281.4 6.5 %collective-permute-done.62 = bf16[128,1024]{1,0:T(8,128)(2,1)S(1)} collective-permute-done((bf16[128,1024]{1,0:T(8,128)(2,1)S(1)}, bf16[128,1024]{1,0:T(8,128)(2,1)S(1)}, u32[]{:S(2)}, u32[]{:S(2)}) %collective-permute-start.62) | collective-permute-done | bytes 262176 | tf_op jit(solution)/shard_map/ppermute | solution.py:47
  295.1 5.0 %widen.1 = (f32[1024,512]{1,0:T(8,128)}, f32[1024,512]{1,0:T(8,128)}, f32[512,1024]{1,0:T(8,128)}) custom-call(bf16[4,768,512]{2,1,0:T(8,128)(2,1)} %bitcast.82), custom_call_target="tpu_custom_call" | custom-call | flops 1000000 | bytes 100000 | tf_op jit(solution)/shard_map/widen/pallas_call | solution.py:652
  (283 shorter events, 142.4 us)
Async XLA Ops:
  7.2 234.9 %reduce-scatter.2.cloned.1.call-start = ((), (), s32[]{:S(2)}) async-start(), calls=%async_computation.1 | async-start | bytes 3932160 | tf_op jit(solution)/shard_map/reduce_scatter | solution.py:828
  12.3 27.4 %collective-permute-start.1 = (bf16[256,1664]{1,0:T(8,128)(2,1)}, bf16[256,1664]{1,0:T(8,128)(2,1)S(1)}, u32[]{:S(2)}, u32[]{:S(2)}) collective-permute-start(bf16[256,1664]{1,0:T(8,128)(2,1)} %get-tuple-element.207), channel_id=1, source_target_pairs={{0,96},{32,0},{64,32},{96,64},{1,97},{33,1},{65,33},{97,65},{2,98}... | collective-permute-start | bytes 2555912 | tf_op jit(solution)/shard_map/ppermute | solution.py:59
  15.6 24.1 %collective-permute-start = (bf16[256,1664]{1,0:T(8,128)(2,1)}, bf16[256,1664]{1,0:T(8,128)(2,1)S(1)}, u32[]{:S(2)}, u32[]{:S(2)}) collective-permute-start(bf16[256,1664]{1,0:T(8,128)(2,1)} %get-tuple-element.207), channel_id=1, source_target_pairs={{0,32},{32,64},{64,96},{96,0},{1,33},{33,65},{65,97},{97,1},{2,34}... | collective-permute-start | bytes 2555912 | tf_op jit(solution)/shard_map/ppermute | solution.py:59
  17.9 15.8 %collective-permute-start.5 = (bf16[256,1024]{1,0:T(8,128)(2,1)}, bf16[256,1024]{1,0:T(8,128)(2,1)S(1)}, u32[]{:S(2)}, u32[]{:S(2)}) collective-permute-start(bf16[256,1024]{1,0:T(8,128)(2,1)} %pad_maximum_fusion.2), channel_id=1, source_target_pairs={{0,24},{1,7},{2,26},{3,1},{4,28},{5,3},{6,30},{7,5},{8,0},{9,15},{... | collective-permute-start | bytes 1572872 | tf_op jit(solution)/shard_map/ppermute | solution.py:47
  22.1 15.5 %collective-permute-start.3 = (bf16[256,1024]{1,0:T(8,128)(2,1)}, bf16[256,1024]{1,0:T(8,128)(2,1)}, u32[]{:S(2)}, u32[]{:S(2)}) collective-permute-start(bf16[256,1024]{1,0:T(8,128)(2,1)} %pad_maximum_fusion.2), channel_id=1, source_target_pairs={{0,8},{1,3},{2,10},{3,5},{4,12},{5,7},{6,14},{7,1},{8,16},{9,11},{... | collective-permute-start | bytes 1572872 | tf_op jit(solution)/shard_map/ppermute | solution.py:47
  39.9 19.2 %collective-permute-start.10 = (bf16[512,1664]{1,0:T(8,128)(2,1)S(1)}, bf16[512,1664]{1,0:T(8,128)(2,1)S(1)}, u32[]{:S(2)}, u32[]{:S(2)}) collective-permute-start(bf16[512,1664]{1,0:T(8,128)(2,1)S(1)} %constant_dynamic-update-slice_fusion.near_ref), channel_id=1, source_target_pairs={{0,1},{1,0},{2,3},{3,2},{4,5},{5,4},{6,7},{7,6},{8,9},{9,8},{10,11... | collective-permute-start | bytes 5111816 | tf_op jit(solution)/shard_map/ppermute | solution.py:55
  42.7 15.4 %collective-permute-start.8 = (bf16[4,128,1024]{2,1,0:T(8,128)(2,1)}, bf16[4,128,1024]{2,1,0:T(8,128)(2,1)S(1)}, u32[]{:S(2)}, u32[]{:S(2)}) collective-permute-start(bf16[4,128,1024]{2,1,0:T(8,128)(2,1)} %pad_maximum_fusion.1.refs_2_), channel_id=1, source_target_pairs={{0,2},{1,9},{2,4},{3,11},{4,6},{5,13},{6,0},{7,15},{8,10},{9,17},{... | collective-permute-start | bytes 3145736 | tf_op jit(solution)/shard_map/ppermute | solution.py:51
  63.1 21.3 %collective-permute-start.12 = (bf16[4,128,1024]{2,1,0:T(8,128)(2,1)}, bf16[4,128,1024]{2,1,0:T(8,128)(2,1)S(1)}, u32[]{:S(2)}, u32[]{:S(2)}) collective-permute-start(bf16[4,128,1024]{2,1,0:T(8,128)(2,1)} %pad_maximum_fusion.1.refs_2_), channel_id=1, source_target_pairs={{0,4},{1,17},{2,6},{3,19},{4,0},{5,21},{6,2},{7,23},{8,12},{9,25},... | collective-permute-start | bytes 3145736 | tf_op jit(solution)/shard_map/ppermute | solution.py:51
  64.0 24.4 %collective-permute-start.20 = (bf16[4,128,1024]{2,1,0:T(8,128)(2,1)}, bf16[4,128,1024]{2,1,0:T(8,128)(2,1)}, u32[]{:S(2)}, u32[]{:S(2)}) collective-permute-start(bf16[4,128,1024]{2,1,0:T(8,128)(2,1)} %pad_maximum_fusion.1.refs_2_), channel_id=1, source_target_pairs={{0,1},{1,0},{2,3},{3,2},{4,5},{5,4},{6,7},{7,6},{8,9},{9,8},{10,11... | collective-permute-start | bytes 3145736 | tf_op jit(solution)/shard_map/ppermute | solution.py:55
  64.7 15.4 %collective-permute-start.15 = (bf16[128,1024]{1,0:T(8,128)(2,1)}, bf16[128,1024]{1,0:T(8,128)(2,1)S(1)}, u32[]{:S(2)}, u32[]{:S(2)}) collective-permute-start(bf16[128,1024]{1,0:T(8,128)(2,1)} %collective-permute-done.2.r1), channel_id=1, source_target_pairs={{0,24},{1,7},{2,26},{3,1},{4,28},{5,3},{6,30},{7,5},{8,0},{9,15},{... | collective-permute-start | bytes 786440 | tf_op jit(solution)/shard_map/ppermute | solution.py:47
  98.2 15.5 %collective-permute-start.23 = (bf16[4,144,1024]{2,1,0:T(8,128)(2,1)S(1)}, bf16[4,144,1024]{2,1,0:T(8,128)(2,1)S(1)}, u32[]{:S(2)}, u32[]{:S(2)}) collective-permute-start(bf16[4,144,1024]{2,1,0:T(8,128)(2,1)S(1)} %pad_maximum_fusion.refs_0_), channel_id=1, source_target_pairs={{0,6},{1,25},{2,0},{3,27},{4,2},{5,29},{6,4},{7,31},{8,14},{9,1},{... | collective-permute-start | bytes 3538952 | tf_op jit(solution)/shard_map/ppermute | solution.py:51
  98.8 16.7 %collective-permute-start.22 = (bf16[4,144,1024]{2,1,0:T(8,128)(2,1)S(1)}, bf16[4,144,1024]{2,1,0:T(8,128)(2,1)}, u32[]{:S(2)}, u32[]{:S(2)}) collective-permute-start(bf16[4,144,1024]{2,1,0:T(8,128)(2,1)S(1)} %pad_maximum_fusion.refs_0_), channel_id=1, source_target_pairs={{0,2},{1,9},{2,4},{3,11},{4,6},{5,13},{6,0},{7,15},{8,10},{9,17},{... | collective-permute-start | bytes 3538952 | tf_op jit(solution)/shard_map/ppermute | solution.py:51
  115.5 17.1 %collective-permute-start.25 = (bf16[4,144,1024]{2,1,0:T(8,128)(2,1)}, bf16[4,144,1024]{2,1,0:T(8,128)(2,1)S(1)}, u32[]{:S(2)}, u32[]{:S(2)}) collective-permute-start(bf16[4,144,1024]{2,1,0:T(8,128)(2,1)} %copy-done.5), channel_id=1, source_target_pairs={{0,4},{1,17},{2,6},{3,19},{4,0},{5,21},{6,2},{7,23},{8,12},{9,25},... | collective-permute-start | bytes 3538952 | tf_op jit(solution)/shard_map/ppermute | solution.py:51
  115.5 17.1 %collective-permute-start.26 = (bf16[4,144,1024]{2,1,0:T(8,128)(2,1)}, bf16[4,144,1024]{2,1,0:T(8,128)(2,1)}, u32[]{:S(2)}, u32[]{:S(2)}) collective-permute-start(bf16[4,144,1024]{2,1,0:T(8,128)(2,1)} %collective-permute-done.22.refs_0_), channel_id=1, source_target_pairs={{0,1},{1,0},{2,3},{3,2},{4,5},{5,4},{6,7},{7,6},{8,9},{9,8},{10,11... | collective-permute-start | bytes 3538952 | tf_op jit(solution)/shard_map/ppermute | solution.py:55
  132.6 19.4 %collective-permute-start.30 = (bf16[4,144,1024]{2,1,0:T(8,128)(2,1)S(1)}, bf16[4,144,1024]{2,1,0:T(8,128)(2,1)S(1)}, u32[]{:S(2)}, u32[]{:S(2)}) collective-permute-start(bf16[4,144,1024]{2,1,0:T(8,128)(2,1)S(1)} %collective-permute-done.25.refs_0_), channel_id=1, source_target_pairs={{0,1},{1,0},{2,3},{3,2},{4,5},{5,4},{6,7},{7,6},{8,9},{9,8},{10,11... | collective-permute-start | bytes 3538952 | tf_op jit(solution)/shard_map/ppermute | solution.py:55
  136.7 15.3 %collective-permute-start.31 = (bf16[256,1024]{1,0:T(8,128)(2,1)S(1)}, bf16[256,1024]{1,0:T(8,128)(2,1)}, u32[]{:S(2)}, u32[]{:S(2)}) collective-permute-start(bf16[256,1024]{1,0:T(8,128)(2,1)S(1)} %pad_maximum_fusion.3.a0), channel_id=1, source_target_pairs={{0,8},{1,3},{2,10},{3,5},{4,12},{5,7},{6,14},{7,1},{8,16},{9,11},{... | collective-permute-start | bytes 1572872 | tf_op jit(solution)/shard_map/ppermute | solution.py:47
  159.0 16.0 %collective-permute-start.38 = (bf16[4,144,1024]{2,1,0:T(8,128)(2,1)}, bf16[4,144,1024]{2,1,0:T(8,128)(2,1)}, u32[]{:S(2)}, u32[]{:S(2)}) collective-permute-start(bf16[4,144,1024]{2,1,0:T(8,128)(2,1)} %get-tuple-element.297), channel_id=1, source_target_pairs={{0,1},{1,0},{2,3},{3,2},{4,5},{5,4},{6,7},{7,6},{8,9},{9,8},{10,11... | collective-permute-start | bytes 3538952 | tf_op jit(solution)/shard_map/ppermute | solution.py:55
  161.3 15.5 %collective-permute-start.36 = (bf16[4,144,1024]{2,1,0:T(8,128)(2,1)S(1)}, bf16[4,144,1024]{2,1,0:T(8,128)(2,1)}, u32[]{:S(2)}, u32[]{:S(2)}) collective-permute-start(bf16[4,144,1024]{2,1,0:T(8,128)(2,1)S(1)} %add_convert_fusion.4), channel_id=1, source_target_pairs={{0,6},{1,25},{2,0},{3,27},{4,2},{5,29},{6,4},{7,31},{8,14},{9,1},{... | collective-permute-start | bytes 3538952 | tf_op jit(solution)/shard_map/ppermute | solution.py:51
  162.2 17.0 %collective-permute-start.37 = (bf16[4,144,1024]{2,1,0:T(8,128)(2,1)S(1)}, bf16[4,144,1024]{2,1,0:T(8,128)(2,1)S(1)}, u32[]{:S(2)}, u32[]{:S(2)}) collective-permute-start(bf16[4,144,1024]{2,1,0:T(8,128)(2,1)S(1)} %add_convert_fusion.3), channel_id=1, source_target_pairs={{0,2},{1,9},{2,4},{3,11},{4,6},{5,13},{6,0},{7,15},{8,10},{9,17},{... | collective-permute-start | bytes 3538952 | tf_op jit(solution)/shard_map/ppermute | solution.py:51
  184.4 16.9 %collective-permute-start.40 = (bf16[4,144,1024]{2,1,0:T(8,128)(2,1)S(1)}, bf16[4,144,1024]{2,1,0:T(8,128)(2,1)S(1)}, u32[]{:S(2)}, u32[]{:S(2)}) collective-permute-start(bf16[4,144,1024]{2,1,0:T(8,128)(2,1)S(1)} %add_convert_fusion.2), channel_id=1, source_target_pairs={{0,4},{1,17},{2,6},{3,19},{4,0},{5,21},{6,2},{7,23},{8,12},{9,25},... | collective-permute-start | bytes 3538952 | tf_op jit(solution)/shard_map/ppermute | solution.py:51
  201.4 87.8 %all-gather.2.cloned.1.call-start = ((), (), s32[]{:S(2)}) async-start(), calls=%async_computation.2 | async-start | bytes 3932160 | tf_op jit(solution)/shard_map/all_gather | solution.py:863
  215.4 15.6 %collective-permute-start.50 = (bf16[4,128,1024]{2,1,0:T(8,128)(2,1)}, bf16[4,128,1024]{2,1,0:T(8,128)(2,1)}, u32[]{:S(2)}, u32[]{:S(2)}) collective-permute-start(bf16[4,128,1024]{2,1,0:T(8,128)(2,1)} %get-tuple-element.349), channel_id=1, source_target_pairs={{0,2},{1,9},{2,4},{3,11},{4,6},{5,13},{6,0},{7,15},{8,10},{9,17},{... | collective-permute-start | bytes 3145736 | tf_op jit(solution)/shard_map/ppermute | solution.py:51
  242.2 15.6 %collective-permute-start.57 = (bf16[4,128,1024]{2,1,0:T(8,128)(2,1)S(1)}, bf16[4,128,1024]{2,1,0:T(8,128)(2,1)}, u32[]{:S(2)}, u32[]{:S(2)}) collective-permute-start(bf16[4,128,1024]{2,1,0:T(8,128)(2,1)S(1)} %add_convert_fusion.6), channel_id=1, source_target_pairs={{0,4},{1,17},{2,6},{3,19},{4,0},{5,21},{6,2},{7,23},{8,12},{9,25},... | collective-permute-start | bytes 3145736 | tf_op jit(solution)/shard_map/ppermute | solution.py:51
  247.9 20.6 %collective-permute-start.56 = (bf16[256,512]{1,0:T(8,128)(2,1)}, bf16[256,512]{1,0:T(8,128)(2,1)S(1)}, u32[]{:S(2)}, u32[]{:S(2)}) collective-permute-start(bf16[256,512]{1,0:T(8,128)(2,1)} %get-tuple-element.365), channel_id=1, source_target_pairs={{0,32},{32,64},{64,96},{96,0},{1,33},{33,65},{65,97},{97,1},{2,34}... | collective-permute-start | bytes 786440 | tf_op jit(solution)/shard_map/ppermute | solution.py:59
  (94 other events, 801.1 us)
Sparse Core Ops, SparseCore 0:
  201.5 33.5 reduce-scatter.1
  242.3 46.8 all-gather.1
where the time goes:
time: 330 us; the launch traced here: 323 us
  Pallas kernels  106 us (32%)
  waiting for transfers between devices  94.2 us (29%)
  starting transfers between devices  69.2 us (21%)
  other arithmetic  23.1 us (7%)
  local copies, waits for them, and re-layouts  15.6 us (5%)
  between operations  15.1 us (5%)
    pallas_call x9, Pallas kernels, run_local(): pl.pallas_call(kernel, in_specs=[pl.BlockSpec(memory_space=pltpu.SMEM)] +...  45 us
    pallas_call x4, Pallas kernels, run_experts(): pl.pallas_call(functools.partial(expert_kernel, len(rows), len(grads)), i...  44.9 us
    ppermute x24, waiting for transfers between devices, along_first(): return lax.ppermute(v, ('y', 'z', 'core'), plane_pairs(k % 4, 0, 0))  38.7 us
    ppermute x15, waiting for transfers between devices, along_second(): return lax.ppermute(v, ('y', 'z', 'core'), plane_pairs(0, k % 4, 0))  28.3 us
    ppermute x24, starting transfers between devices, along_first(): return lax.ppermute(v, ('y', 'z', 'core'), plane_pairs(k % 4, 0, 0))  24.9 us
    ppermute x22, starting transfers between devices, swap_core(): return lax.ppermute(v, 'core', [(0, 1), (1, 0)])  23.9 us
    ppermute x7, waiting for transfers between devices, along_x(): return lax.ppermute(v, 'x', [(i, (i + k) % 4) for i in range(4)])  20.7 us
    ppermute x15, starting transfers between devices, along_second(): return lax.ppermute(v, ('y', 'z', 'core'), plane_pairs(0, k % 4, 0))  12.8 us
  transfers between devices with their start and end apart: 70, of which 31 were waited for; matrix products, arithmetic and copies ran while one was open for 8% of the time, Pallas kernels for 30%

commit v1 on v0

--- a/solution.py
+++ b/solution.py
@@ -243,7 +243,7 @@
             pltpu.SemaphoreType.DMA((5,)),
             pltpu.SemaphoreType.DMA((3,)),
         ],
-        compiler_params=pltpu.CompilerParams(vmem_limit_bytes=60 * 1024 * 1024),
+        compiler_params=pltpu.CompilerParams(vmem_limit_bytes=56 * 1024 * 1024),
         cost_estimate=SHORT,
         name="experts",
     )(place, *rows, *grads, gate, up, down)
@@ -299,7 +299,7 @@
             pltpu.SemaphoreType.DMA((4, 5)),
             pltpu.SemaphoreType.DMA((4,)),
         ],
-        compiler_params=pltpu.CompilerParams(vmem_limit_bytes=60 * 1024 * 1024),
+        compiler_params=pltpu.CompilerParams(vmem_limit_bytes=56 * 1024 * 1024),
         cost_estimate=SHORT,
         name="expert_weight_grads",
     )(*operands)
@@ -635,8 +635,8 @@
         out_ref[:, pl.ds(pl.multiple_of(side * 512, 512), 512)] = ref[:, D:SMALL_AT].astype(f32)
     tiny = own_ref[:, SMALL_AT:SMALL_AT + 128].astype(f32)
     tiny = tiny + other_ref[:, SMALL_AT:SMALL_AT + 128].astype(f32)
-    router_ref[...] = tiny[:, 0:EXPERTS]
     turned = tiny.T
+    router_ref[...] = turned[0:EXPERTS]
     one_ref[...] = turned[32:33]
     two_ref[...] = turned[33:34]
 
@@ -663,7 +663,7 @@
             jax.ShapeDtypeStruct((D, FFE), f32),
             jax.ShapeDtypeStruct((FFE, D), f32),
         ],
-        compiler_params=pltpu.CompilerParams(vmem_limit_bytes=60 * 1024 * 1024),
+        compiler_params=pltpu.CompilerParams(vmem_limit_bytes=56 * 1024 * 1024),
         cost_estimate=SHORT,
         name="widen",
     )(sums)
@@ -888,7 +888,7 @@
     qkv_grad, out_grad, router_grad, gain_one, gain_two = run_local(
         finish_kernel, "finish", place, [both, swap_core(both)],
         [
-            ((256, 2 * D), f32), ((256, D), f32), ((256, EXPERTS), f32),
+            ((256, 2 * D), f32), ((256, D), f32), ((EXPERTS, 256), f32),
             ((1, 256), f32), ((1, 256), f32),
         ],
         [],
@@ -901,7 +901,7 @@
         qkv_grad,
         out_grad,
         gain_two.reshape(256),
-        router_grad,
+        router_grad.T,
         gate_total[None],
         up_total[None],
         down_total[None],

time: 330 us -> 326 us (0.988)
    unnamed x100 -> x103, local copies, waits for them, and re-layouts: 9.08 us -> 6.12 us
  transfers between devices with their start and end apart: 70 -> 70, of which waited for: 31 -> 31; matrix products, arithmetic and copies ran while one was open for 8% -> 7% of each run, Pallas kernels for 30% -> 31%
where the time goes in v1:
time: 326 us; the launch traced here: 320 us
  Pallas kernels  106 us (33%)
  waiting for transfers between devices  97.1 us (30%)
  starting transfers between devices  68.7 us (21%)
  other arithmetic  20.2 us (6%)
  between operations  15.1 us (5%)
  local copies, waits for them, and re-layouts  12.8 us (4%)
    pallas_call x9, Pallas kernels, run_local(): pl.pallas_call(kernel, in_specs=[pl.BlockSpec(memory_space=pltpu.SMEM)] +...  45 us
    pallas_call x4, Pallas kernels, run_experts(): pl.pallas_call(functools.partial(expert_kernel, len(rows), len(grads)), i...  44.8 us
    ppermute x24, waiting for transfers between devices, along_first(): return lax.ppermute(v, ('y', 'z', 'core'), plane_pairs(k % 4, 0, 0))  38.7 us
    ppermute x15, waiting for transfers between devices, along_second(): return lax.ppermute(v, ('y', 'z', 'core'), plane_pairs(0, k % 4, 0))  30.5 us
    ppermute x24, starting transfers between devices, along_first(): return lax.ppermute(v, ('y', 'z', 'core'), plane_pairs(k % 4, 0, 0))  24.4 us
    ppermute x22, starting transfers between devices, swap_core(): return lax.ppermute(v, 'core', [(0, 1), (1, 0)])  23.7 us
    ppermute x7, waiting for transfers between devices, along_x(): return lax.ppermute(v, 'x', [(i, (i + k) % 4) for i in range(4)])  21 us
    ppermute x15, starting transfers between devices, along_second(): return lax.ppermute(v, ('y', 'z', 'core'), plane_pairs(0, k % 4, 0))  12.8 us
  transfers between devices with their start and end apart: 70, of which 31 were waited for; matrix products, arithmetic and copies ran while one was open for 7% of the time, Pallas kernels for 31%

profile of v1, /device:TPU:1, one launch (start us, length us, event | category | flops | bytes accessed | tf_op | source)
XLA Modules:
  0.0 319.5 jit_solution(10088012647689958888)
XLA Ops:
  12.3 3.3 %collective-permute-start.1 = (bf16[256,1664]{1,0:T(8,128)(2,1)}, bf16[256,1664]{1,0:T(8,128)(2,1)S(1)}, u32[]{:S(2)}, u32[]{:S(2)}) collective-permute-start(bf16[256,1664]{1,0:T(8,128)(2,1)} %get-tuple-element.207), channel_id=1, source_target_pairs={{0,96},{32,0},{64,32},{96,64},{1,97},{33,1},{65,33},{97,65},{2,98}... | collective-permute-start | bytes 2555912 | tf_op jit(solution)/shard_map/ppermute | solution.py:59
  17.9 3.8 %collective-permute-start.5 = (bf16[256,1024]{1,0:T(8,128)(2,1)}, bf16[256,1024]{1,0:T(8,128)(2,1)S(1)}, u32[]{:S(2)}, u32[]{:S(2)}) collective-permute-start(bf16[256,1024]{1,0:T(8,128)(2,1)} %pad_maximum_fusion.2), channel_id=1, source_target_pairs={{0,24},{1,7},{2,26},{3,1},{4,28},{5,3},{6,30},{7,5},{8,0},{9,15},{... | collective-permute-start | bytes 1572872 | tf_op jit(solution)/shard_map/ppermute | solution.py:47
  24.2 9.5 %collective-permute-done.5.r6 = bf16[256,1024]{1,0:T(8,128)(2,1)S(1)} collective-permute-done((bf16[256,1024]{1,0:T(8,128)(2,1)}, bf16[256,1024]{1,0:T(8,128)(2,1)S(1)}, u32[]{:S(2)}, u32[]{:S(2)}) %collective-permute-start.5) | collective-permute-done | bytes 524320 | tf_op jit(solution)/shard_map/ppermute | solution.py:47
  33.8 3.8 %collective-permute-done.3.r2 = bf16[256,1024]{1,0:T(8,128)(2,1)} collective-permute-done((bf16[256,1024]{1,0:T(8,128)(2,1)}, bf16[256,1024]{1,0:T(8,128)(2,1)}, u32[]{:S(2)}, u32[]{:S(2)}) %collective-permute-start.3) | collective-permute-done | bytes 524320 | tf_op jit(solution)/shard_map/ppermute | solution.py:47
  45.7 6.9 %collective-permute-done.7 = bf16[128,1664]{1,0:T(8,128)(2,1)S(1)} collective-permute-done((bf16[128,1664]{1,0:T(8,128)(2,1)S(1)}, bf16[128,1664]{1,0:T(8,128)(2,1)S(1)}, u32[]{:S(2)}, u32[]{:S(2)}) %collective-permute-start.7) | collective-permute-done | bytes 426016 | tf_op jit(solution)/shard_map/ppermute | solution.py:59
  67.1 5.1 %project.1 = (bf16[128,1024]{1,0:T(8,128)(2,1)}, bf16[128,1024]{1,0:T(8,128)(2,1)}, f32[40,1024]{1,0:T(8,128)}) custom-call(s32[5]{0:T(128)} %stack.59.place_ref, bf16[128,1024]{1,0:T(8,128)(2,1)} %bitcast.77, bf16[256,2048]{1,0:T(8,128)(2,1)} %mine_ref.7, bf16[256,128]{1,0:T(8,128)(2,1)} %get-tuple-element.206.tiny_ref, f32[128,384]{1,0:T(8,128)} %concatenate.25.table_ref, ...), custom_call_target="tpu_custom_call" | custom-call | flops 1000000 | bytes 100000 | tf_op jit(solution)/shard_map/project/pallas_call | solution.py:675
  72.2 6.8 %attend.1 = (bf16[128,1024]{1,0:T(8,128)(2,1)}, f32[128,1024]{1,0:T(8,128)}, f32[128,32]{1,0:T(8,128)}, bf16[144,1024]{1,0:T(8,128)(2,1)}) custom-call(s32[5]{0:T(128)} %stack.59.place_ref, bf16[128,1024]{1,0:T(8,128)(2,1)} %bitcast.78, bf16[128,1024]{1,0:T(8,128)(2,1)} %get-tuple-element.216.q_ref, bf16[128,1024]{1,0:T(8,128)(2,1)} %get-tuple-element.217.kv_ref, ...), custom_call_target="tpu_custom_call" | custom-call | flops 1000000 | bytes 100000 | tf_op jit(solution)/shard_map/attend/pallas_call | solution.py:675
  79.9 3.6 %collective-permute-done.12.refs_2_ = bf16[4,128,1024]{2,1,0:T(8,128)(2,1)S(1)} collective-permute-done((bf16[4,128,1024]{2,1,0:T(8,128)(2,1)}, bf16[4,128,1024]{2,1,0:T(8,128)(2,1)S(1)}, u32[]{:S(2)}, u32[]{:S(2)}) %collective-permute-start.12) | collective-permute-done | bytes 1048608 | tf_op jit(solution)/shard_map/ppermute | solution.py:51
  100.9 11.2 %experts.4 = (bf16[4,144,1024]{2,1,0:T(8,128)(2,1)}, bf16[4,144,1024]{2,1,0:T(8,128)(2,1)}, bf16[4,128,1024]{2,1,0:T(8,128)(2,1)}, bf16[4,128,1024]{2,1,0:T(8,12...) custom-call(s32[5]{0:T(128)} %stack.59.place_ref, ...), custom_call_target="tpu_custom_call" | custom-call | flops 1000000 | bytes 100000 | tf_op jit(solution)/shard_map/experts/pallas_call | solution.py:215
  118.2 11.2 %experts.5 = (bf16[4,144,1024]{2,1,0:T(8,128)(2,1)}, bf16[4,144,1024]{2,1,0:T(8,128)(2,1)}, bf16[4,128,1024]{2,1,0:T(8,128)(2,1)}, bf16[4,128,1024]{2,1,0:T(8,12...) custom-call(s32[5]{0:T(128)} %stack.59.place_ref, ...), custom_call_target="tpu_custom_call" | custom-call | flops 1000000 | bytes 100000 | tf_op jit(solution)/shard_map/experts/pallas_call | solution.py:215
  131.5 3.9 %collective-permute-start.30 = (bf16[4,144,1024]{2,1,0:T(8,128)(2,1)S(1)}, bf16[4,144,1024]{2,1,0:T(8,128)(2,1)S(1)}, u32[]{:S(2)}, u32[]{:S(2)}) collective-permute-start(bf16[4,144,1024]{2,1,0:T(8,128)(2,1)S(1)} %collective-permute-done.25.refs_0_), channel_id=1, source_target_pairs={{0,1},{1,0},{2,3},{3,2},{4,5},{5,4},{6,7},{7,6},{8,9},{9,8},{10,11... | collective-permute-start | bytes 3538952 | tf_op jit(solution)/shard_map/ppermute | solution.py:55
  136.8 11.2 %experts.6 = (bf16[4,144,1024]{2,1,0:T(8,128)(2,1)}, bf16[4,144,1024]{2,1,0:T(8,128)(2,1)}, bf16[4,128,1024]{2,1,0:T(8,128)(2,1)}, bf16[4,128,1024]{2,1,0:T(8,12...) custom-call(s32[5]{0:T(128)} %stack.59.place_ref, ...), custom_call_target="tpu_custom_call" | custom-call | flops 1000000 | bytes 100000 | tf_op jit(solution)/shard_map/experts/pallas_call | solution.py:215
  153.6 4.5 %norm_line.1.n_ref = bf16[1024,1024]{1,0:T(8,128)(2,1)} custom-call(s32[5]{0:T(128)} %stack.59.place_ref, bf16[128,1024]{1,0:T(8,128)(2,1)} %bitcast.79, bf16[128,1024]{1,0:T(8,128)(2,1)} %collective-permute-done.2.r1, bf16[256,1024]{1,0:T(8,128)(2,1)} %collective-permute-done.3.r2, bf16[128,1024]{1,0:T(8,128)(2,1)} %collective-permute-done.13.r3, ...), custom_call_target="tpu_custom_call" | custom-call | flops 1000000 | bytes 100000 | tf_op jit(solution)/shard_map/norm_line/pallas_call | solution.py:675
  161.5 11.2 %experts.7 = (bf16[4,144,1024]{2,1,0:T(8,128)(2,1)}, bf16[4,144,1024]{2,1,0:T(8,128)(2,1)}, bf16[4,128,1024]{2,1,0:T(8,128)(2,1)}, bf16[4,128,1024]{2,1,0:T(8,12...) custom-call(s32[5]{0:T(128)} %stack.59.place_ref, ...), custom_call_target="tpu_custom_call" | custom-call | flops 1000000 | bytes 100000 | tf_op jit(solution)/shard_map/experts/pallas_call | solution.py:215
  184.8 11.0 %expert_weight_grads.1 = bf16[4,768,512]{2,1,0:T(8,128)(2,1)} custom-call(bf16[384,1024]{1,0:T(8,128)(2,1)} %get-tuple-element.301.refs_0_, bf16[384,1024]{1,0:T(8,128)(2,1)} %get-tuple-element.302.refs_1_, bf16[384,1024]{1,0:T(8,128)(2,1)} %get-tuple-element.303.refs_2_, bf16[384,1024]{1,0:T(8,128)(2,1)} %get-tuple-element.304.refs_3_, ...), custom_call_target="tpu_custom_call" | custom-call | flops 1000000 | bytes 100000 | tf_op jit(solution)/shard_map/expert_weight_grads/pallas_call | solution.py:287
  195.8 3.6 %collective-permute-done.40 = bf16[4,144,1024]{2,1,0:T(8,128)(2,1)S(1)} collective-permute-done((bf16[4,144,1024]{2,1,0:T(8,128)(2,1)S(1)}, bf16[4,144,1024]{2,1,0:T(8,128)(2,1)S(1)}, u32[]{:S(2)}, u32[]{:S(2)}) %collective-permute-start.40) | collective-permute-done | bytes 1179680 | tf_op jit(solution)/shard_map/ppermute | solution.py:51
  204.8 3.9 %add_convert_fusion.7 = (bf16[4,128,1024]{2,1,0:T(8,128)(2,1)}, bf16[4,128,1024]{2,1,0:T(8,128)(2,1)}) fusion(bf16[4,128,1024]{2,1,0:T(8,128)(2,1)} %collective-permute-done.42, bf16[4,128,1024]{2,1,0:T(8,128)(2,1)S(1)} %copy-done.27, bf16[4,128,1024]{2,1,0:T(8,128)(2,1)} %collective-permute-done.41, bf16[4,128,1024]{2,1,0:T(8,128)(2,1)S(1)} %copy-done.26), kind=kLoop, calls=%fused_computation.7 | loop fusion | flops 4194304 | bytes 6291456 | tf_op jit(solution)/shard_map/convert_element_type | solution.py:832
  214.7 9.7 %attend_back.1 = (bf16[4,128,384]{2,1,0:T(8,128)(2,1)}, bf16[4,128,384]{2,1,0:T(8,128)(2,1)}, f32[128,1024]{1,0:T(8,128)}, f32[40,1024]{1,0:T(8,128)}) custom-call(s32[5]{0:T(128)} %stack.59.place_ref, bf16[144,1024]{1,0:T(8,128)(2,1)} %get-tuple-element.407.b0, bf16[144,1024]{1,0:T(8,128)(2,1)} %copy-done.37, bf16[144,1024]{1,0:T(8,128)(2,1)} %copy-done.35, ...), custom_call_target="tpu_custom_call" | custom-call | flops 1000000 | bytes 100000 | tf_op jit(solution)/shard_map/attend_back/pallas_call | solution.py:675
  233.8 6.2 %input_back.1 = (f32[128,1024]{1,0:T(8,128)}, f32[40,1024]{1,0:T(8,128)}) custom-call(s32[5]{0:T(128)} %stack.59.place_ref, bf16[4,128,384]{2,1,0:T(8,128)(2,1)} %get-tuple-element.350.mine_grad.g0, bf16[4,128,384]{2,1,0:T(8,128)(2,1)} %get-tuple-element.352.other_grad, bf16[256,2048]{1,0:T(8,128)(2,1)} %mine_ref.7, bf16[128,1024]{1,0:T(8,128)(2,1)} %bitcast.80, ...), custom_call_target="tpu_custom_call" | custom-call | flops 1000000 | bytes 100000 | tf_op jit(solution)/shard_map/input_back/pallas_call | solution.py:675
  240.8 4.9 %attention_weights.1 = (bf16[256,512]{1,0:T(8,128)(2,1)}, bf16[256,512]{1,0:T(8,128)(2,1)}, bf16[256,512]{1,0:T(8,128)(2,1)}, bf16[256,512]{1,0:T(8,128)(2,1)}) custom-call(s32[5]{0:T(128)} %stack.59.place_ref, bf16[1024,1024]{1,0:T(8,128)(2,1)} %norm_line.1.n_ref, bf16[256,1024]{1,0:T(8,128)(2,1)} %copy-done.8, bf16[256,1024]{1,0:T(8,128)(2,1)} %copy-done.33, ...), custom_call_target="tpu_custom_call" | custom-call | flops 1000000 | bytes 100000 | tf_op jit(solution)/shard_map/attention_weights/pallas_call | solution.py:675
  247.2 8.6 %collective-permute-done.57 = bf16[4,128,1024]{2,1,0:T(8,128)(2,1)} collective-permute-done((bf16[4,128,1024]{2,1,0:T(8,128)(2,1)S(1)}, bf16[4,128,1024]{2,1,0:T(8,128)(2,1)}, u32[]{:S(2)}, u32[]{:S(2)}) %collective-permute-start.57) | collective-permute-done | bytes 1048608 | tf_op jit(solution)/shard_map/ppermute | solution.py:51
  255.7 10.9 %collective-permute-done.56 = bf16[256,512]{1,0:T(8,128)(2,1)S(1)} collective-permute-done((bf16[256,512]{1,0:T(8,128)(2,1)}, bf16[256,512]{1,0:T(8,128)(2,1)S(1)}, u32[]{:S(2)}, u32[]{:S(2)}) %collective-permute-start.56) | collective-permute-done | bytes 262176 | tf_op jit(solution)/shard_map/ppermute | solution.py:59
  279.4 6.5 %collective-permute-done.62 = bf16[128,1024]{1,0:T(8,128)(2,1)S(1)} collective-permute-done((bf16[128,1024]{1,0:T(8,128)(2,1)S(1)}, bf16[128,1024]{1,0:T(8,128)(2,1)S(1)}, u32[]{:S(2)}, u32[]{:S(2)}) %collective-permute-start.62) | collective-permute-done | bytes 262176 | tf_op jit(solution)/shard_map/ppermute | solution.py:47
  293.0 5.0 %widen.1 = (f32[1024,512]{1,0:T(8,128)}, f32[1024,512]{1,0:T(8,128)}, f32[512,1024]{1,0:T(8,128)}) custom-call(bf16[4,768,512]{2,1,0:T(8,128)(2,1)} %bitcast.83), custom_call_target="tpu_custom_call" | custom-call | flops 1000000 | bytes 100000 | tf_op jit(solution)/shard_map/widen/pallas_call | solution.py:652
  (286 shorter events, 138.3 us)
Async XLA Ops:
  7.2 232.8 %reduce-scatter.2.cloned.1.call-start = ((), (), s32[]{:S(2)}) async-start(), calls=%async_computation.1 | async-start | bytes 3932160 | tf_op jit(solution)/shard_map/reduce_scatter | solution.py:828
  12.3 27.4 %collective-permute-start.1 = (bf16[256,1664]{1,0:T(8,128)(2,1)}, bf16[256,1664]{1,0:T(8,128)(2,1)S(1)}, u32[]{:S(2)}, u32[]{:S(2)}) collective-permute-start(bf16[256,1664]{1,0:T(8,128)(2,1)} %get-tuple-element.207), channel_id=1, source_target_pairs={{0,96},{32,0},{64,32},{96,64},{1,97},{33,1},{65,33},{97,65},{2,98}... | collective-permute-start | bytes 2555912 | tf_op jit(solution)/shard_map/ppermute | solution.py:59
  15.7 24.1 %collective-permute-start = (bf16[256,1664]{1,0:T(8,128)(2,1)}, bf16[256,1664]{1,0:T(8,128)(2,1)S(1)}, u32[]{:S(2)}, u32[]{:S(2)}) collective-permute-start(bf16[256,1664]{1,0:T(8,128)(2,1)} %get-tuple-element.207), channel_id=1, source_target_pairs={{0,32},{32,64},{64,96},{96,0},{1,33},{33,65},{65,97},{97,1},{2,34}... | collective-permute-start | bytes 2555912 | tf_op jit(solution)/shard_map/ppermute | solution.py:59
  17.9 15.8 %collective-permute-start.5 = (bf16[256,1024]{1,0:T(8,128)(2,1)}, bf16[256,1024]{1,0:T(8,128)(2,1)S(1)}, u32[]{:S(2)}, u32[]{:S(2)}) collective-permute-start(bf16[256,1024]{1,0:T(8,128)(2,1)} %pad_maximum_fusion.2), channel_id=1, source_target_pairs={{0,24},{1,7},{2,26},{3,1},{4,28},{5,3},{6,30},{7,5},{8,0},{9,15},{... | collective-permute-start | bytes 1572872 | tf_op jit(solution)/shard_map/ppermute | solution.py:47
  22.2 15.5 %collective-permute-start.3 = (bf16[256,1024]{1,0:T(8,128)(2,1)}, bf16[256,1024]{1,0:T(8,128)(2,1)}, u32[]{:S(2)}, u32[]{:S(2)}) collective-permute-start(bf16[256,1024]{1,0:T(8,128)(2,1)} %pad_maximum_fusion.2), channel_id=1, source_target_pairs={{0,8},{1,3},{2,10},{3,5},{4,12},{5,7},{6,14},{7,1},{8,16},{9,11},{... | collective-permute-start | bytes 1572872 | tf_op jit(solution)/shard_map/ppermute | solution.py:47
  39.9 18.3 %collective-permute-start.10 = (bf16[512,1664]{1,0:T(8,128)(2,1)S(1)}, bf16[512,1664]{1,0:T(8,128)(2,1)S(1)}, u32[]{:S(2)}, u32[]{:S(2)}) collective-permute-start(bf16[512,1664]{1,0:T(8,128)(2,1)S(1)} %constant_dynamic-update-slice_fusion.near_ref), channel_id=1, source_target_pairs={{0,1},{1,0},{2,3},{3,2},{4,5},{5,4},{6,7},{7,6},{8,9},{9,8},{10,11... | collective-permute-start | bytes 5111816 | tf_op jit(solution)/shard_map/ppermute | solution.py:55
  40.7 15.1 %collective-permute-start.9 = (bf16[4,128,1024]{2,1,0:T(8,128)(2,1)}, bf16[4,128,1024]{2,1,0:T(8,128)(2,1)}, u32[]{:S(2)}, u32[]{:S(2)}) collective-permute-start(bf16[4,128,1024]{2,1,0:T(8,128)(2,1)} %pad_maximum_fusion.1.refs_2_), channel_id=1, source_target_pairs={{0,6},{1,25},{2,0},{3,27},{4,2},{5,29},{6,4},{7,31},{8,14},{9,1},{... | collective-permute-start | bytes 3145736 | tf_op jit(solution)/shard_map/ppermute | solution.py:51
  42.7 15.5 %collective-permute-start.8 = (bf16[4,128,1024]{2,1,0:T(8,128)(2,1)}, bf16[4,128,1024]{2,1,0:T(8,128)(2,1)}, u32[]{:S(2)}, u32[]{:S(2)}) collective-permute-start(bf16[4,128,1024]{2,1,0:T(8,128)(2,1)} %pad_maximum_fusion.1.refs_2_), channel_id=1, source_target_pairs={{0,2},{1,9},{2,4},{3,11},{4,6},{5,13},{6,0},{7,15},{8,10},{9,17},{... | collective-permute-start | bytes 3145736 | tf_op jit(solution)/shard_map/ppermute | solution.py:51
  62.2 21.3 %collective-permute-start.12 = (bf16[4,128,1024]{2,1,0:T(8,128)(2,1)}, bf16[4,128,1024]{2,1,0:T(8,128)(2,1)S(1)}, u32[]{:S(2)}, u32[]{:S(2)}) collective-permute-start(bf16[4,128,1024]{2,1,0:T(8,128)(2,1)} %pad_maximum_fusion.1.refs_2_), channel_id=1, source_target_pairs={{0,4},{1,17},{2,6},{3,19},{4,0},{5,21},{6,2},{7,23},{8,12},{9,25},... | collective-permute-start | bytes 3145736 | tf_op jit(solution)/shard_map/ppermute | solution.py:51
  63.1 24.3 %collective-permute-start.20 = (bf16[4,128,1024]{2,1,0:T(8,128)(2,1)}, bf16[4,128,1024]{2,1,0:T(8,128)(2,1)}, u32[]{:S(2)}, u32[]{:S(2)}) collective-permute-start(bf16[4,128,1024]{2,1,0:T(8,128)(2,1)} %pad_maximum_fusion.1.refs_2_), channel_id=1, source_target_pairs={{0,1},{1,0},{2,3},{3,2},{4,5},{5,4},{6,7},{7,6},{8,9},{9,8},{10,11... | collective-permute-start | bytes 3145736 | tf_op jit(solution)/shard_map/ppermute | solution.py:55
  63.7 15.4 %collective-permute-start.15 = (bf16[128,1024]{1,0:T(8,128)(2,1)}, bf16[128,1024]{1,0:T(8,128)(2,1)S(1)}, u32[]{:S(2)}, u32[]{:S(2)}) collective-permute-start(bf16[128,1024]{1,0:T(8,128)(2,1)} %collective-permute-done.2.r1), channel_id=1, source_target_pairs={{0,24},{1,7},{2,26},{3,1},{4,28},{5,3},{6,30},{7,5},{8,0},{9,15},{... | collective-permute-start | bytes 786440 | tf_op jit(solution)/shard_map/ppermute | solution.py:47
  97.3 15.3 %collective-permute-start.23 = (bf16[4,144,1024]{2,1,0:T(8,128)(2,1)S(1)}, bf16[4,144,1024]{2,1,0:T(8,128)(2,1)S(1)}, u32[]{:S(2)}, u32[]{:S(2)}) collective-permute-start(bf16[4,144,1024]{2,1,0:T(8,128)(2,1)S(1)} %pad_maximum_fusion.refs_0_), channel_id=1, source_target_pairs={{0,6},{1,25},{2,0},{3,27},{4,2},{5,29},{6,4},{7,31},{8,14},{9,1},{... | collective-permute-start | bytes 3538952 | tf_op jit(solution)/shard_map/ppermute | solution.py:51
  97.8 16.6 %collective-permute-start.22 = (bf16[4,144,1024]{2,1,0:T(8,128)(2,1)S(1)}, bf16[4,144,1024]{2,1,0:T(8,128)(2,1)S(1)}, u32[]{:S(2)}, u32[]{:S(2)}) collective-permute-start(bf16[4,144,1024]{2,1,0:T(8,128)(2,1)S(1)} %pad_maximum_fusion.refs_0_), channel_id=1, source_target_pairs={{0,2},{1,9},{2,4},{3,11},{4,6},{5,13},{6,0},{7,15},{8,10},{9,17},{... | collective-permute-start | bytes 3538952 | tf_op jit(solution)/shard_map/ppermute | solution.py:51
  114.4 17.1 %collective-permute-start.25 = (bf16[4,144,1024]{2,1,0:T(8,128)(2,1)}, bf16[4,144,1024]{2,1,0:T(8,128)(2,1)S(1)}, u32[]{:S(2)}, u32[]{:S(2)}) collective-permute-start(bf16[4,144,1024]{2,1,0:T(8,128)(2,1)} %copy-done.5), channel_id=1, source_target_pairs={{0,4},{1,17},{2,6},{3,19},{4,0},{5,21},{6,2},{7,23},{8,12},{9,25},... | collective-permute-start | bytes 3538952 | tf_op jit(solution)/shard_map/ppermute | solution.py:51
  114.4 17.0 %collective-permute-start.26 = (bf16[4,144,1024]{2,1,0:T(8,128)(2,1)S(1)}, bf16[4,144,1024]{2,1,0:T(8,128)(2,1)S(1)}, u32[]{:S(2)}, u32[]{:S(2)}) collective-permute-start(bf16[4,144,1024]{2,1,0:T(8,128)(2,1)S(1)} %collective-permute-done.22.refs_0_), channel_id=1, source_target_pairs={{0,1},{1,0},{2,3},{3,2},{4,5},{5,4},{6,7},{7,6},{8,9},{9,8},{10,11... | collective-permute-start | bytes 3538952 | tf_op jit(solution)/shard_map/ppermute | solution.py:55
  131.5 19.3 %collective-permute-start.30 = (bf16[4,144,1024]{2,1,0:T(8,128)(2,1)S(1)}, bf16[4,144,1024]{2,1,0:T(8,128)(2,1)S(1)}, u32[]{:S(2)}, u32[]{:S(2)}) collective-permute-start(bf16[4,144,1024]{2,1,0:T(8,128)(2,1)S(1)} %collective-permute-done.25.refs_0_), channel_id=1, source_target_pairs={{0,1},{1,0},{2,3},{3,2},{4,5},{5,4},{6,7},{7,6},{8,9},{9,8},{10,11... | collective-permute-start | bytes 3538952 | tf_op jit(solution)/shard_map/ppermute | solution.py:55
  135.6 15.1 %collective-permute-start.31 = (bf16[256,1024]{1,0:T(8,128)(2,1)S(1)}, bf16[256,1024]{1,0:T(8,128)(2,1)S(1)}, u32[]{:S(2)}, u32[]{:S(2)}) collective-permute-start(bf16[256,1024]{1,0:T(8,128)(2,1)S(1)} %pad_maximum_fusion.3.a0), channel_id=1, source_target_pairs={{0,8},{1,3},{2,10},{3,5},{4,12},{5,7},{6,14},{7,1},{8,16},{9,11},{... | collective-permute-start | bytes 1572872 | tf_op jit(solution)/shard_map/ppermute | solution.py:47
  159.0 15.4 %collective-permute-start.36 = (bf16[4,144,1024]{2,1,0:T(8,128)(2,1)S(1)}, bf16[4,144,1024]{2,1,0:T(8,128)(2,1)S(1)}, u32[]{:S(2)}, u32[]{:S(2)}) collective-permute-start(bf16[4,144,1024]{2,1,0:T(8,128)(2,1)S(1)} %add_convert_fusion.4), channel_id=1, source_target_pairs={{0,6},{1,25},{2,0},{3,27},{4,2},{5,29},{6,4},{7,31},{8,14},{9,1},{... | collective-permute-start | bytes 3538952 | tf_op jit(solution)/shard_map/ppermute | solution.py:51
  159.9 17.0 %collective-permute-start.37 = (bf16[4,144,1024]{2,1,0:T(8,128)(2,1)S(1)}, bf16[4,144,1024]{2,1,0:T(8,128)(2,1)S(1)}, u32[]{:S(2)}, u32[]{:S(2)}) collective-permute-start(bf16[4,144,1024]{2,1,0:T(8,128)(2,1)S(1)} %add_convert_fusion.3), channel_id=1, source_target_pairs={{0,2},{1,9},{2,4},{3,11},{4,6},{5,13},{6,0},{7,15},{8,10},{9,17},{... | collective-permute-start | bytes 3538952 | tf_op jit(solution)/shard_map/ppermute | solution.py:51
  182.6 16.9 %collective-permute-start.40 = (bf16[4,144,1024]{2,1,0:T(8,128)(2,1)S(1)}, bf16[4,144,1024]{2,1,0:T(8,128)(2,1)S(1)}, u32[]{:S(2)}, u32[]{:S(2)}) collective-permute-start(bf16[4,144,1024]{2,1,0:T(8,128)(2,1)S(1)} %add_convert_fusion.2), channel_id=1, source_target_pairs={{0,4},{1,17},{2,6},{3,19},{4,0},{5,21},{6,2},{7,23},{8,12},{9,25},... | collective-permute-start | bytes 3538952 | tf_op jit(solution)/shard_map/ppermute | solution.py:51
  199.5 87.7 %all-gather.2.cloned.1.call-start = ((), (), s32[]{:S(2)}) async-start(), calls=%async_computation.2 | async-start | bytes 3932160 | tf_op jit(solution)/shard_map/all_gather | solution.py:863
  213.5 15.6 %collective-permute-start.50 = (bf16[4,128,1024]{2,1,0:T(8,128)(2,1)}, bf16[4,128,1024]{2,1,0:T(8,128)(2,1)}, u32[]{:S(2)}, u32[]{:S(2)}) collective-permute-start(bf16[4,128,1024]{2,1,0:T(8,128)(2,1)} %get-tuple-element.349), channel_id=1, source_target_pairs={{0,2},{1,9},{2,4},{3,11},{4,6},{5,13},{6,0},{7,15},{8,10},{9,17},{... | collective-permute-start | bytes 3145736 | tf_op jit(solution)/shard_map/ppermute | solution.py:51
  240.1 15.6 %collective-permute-start.57 = (bf16[4,128,1024]{2,1,0:T(8,128)(2,1)S(1)}, bf16[4,128,1024]{2,1,0:T(8,128)(2,1)}, u32[]{:S(2)}, u32[]{:S(2)}) collective-permute-start(bf16[4,128,1024]{2,1,0:T(8,128)(2,1)S(1)} %add_convert_fusion.6), channel_id=1, source_target_pairs={{0,4},{1,17},{2,6},{3,19},{4,0},{5,21},{6,2},{7,23},{8,12},{9,25},... | collective-permute-start | bytes 3145736 | tf_op jit(solution)/shard_map/ppermute | solution.py:51
  245.9 20.7 %collective-permute-start.56 = (bf16[256,512]{1,0:T(8,128)(2,1)}, bf16[256,512]{1,0:T(8,128)(2,1)S(1)}, u32[]{:S(2)}, u32[]{:S(2)}) collective-permute-start(bf16[256,512]{1,0:T(8,128)(2,1)} %get-tuple-element.365), channel_id=1, source_target_pairs={{0,32},{32,64},{64,96},{96,0},{1,33},{33,65},{65,97},{97,1},{2,34}... | collective-permute-start | bytes 786440 | tf_op jit(solution)/shard_map/ppermute | solution.py:59
  (96 other events, 793.4 us)
Sparse Core Ops, SparseCore 0:
  199.6 33.1 reduce-scatter.1
  240.2 46.9 all-gather.1
